TPU v7x, 256 devices: a whole 4x4x8 slice. The times are simulated.
256 devices in a mesh: row: 16 (over y_hi, x, core), rep: 16 (over y_lo, z).
Axes of the slice: x: 4, y: 4 (y_hi: 2, y_lo: 2; y = y_hi * 2 + y_lo), z: 8, core: 2. Of those that a mesh axis runs over, the one named last changes fastest.
Arguments:
- features: bfloat16 [65536, 512], P(('row', 'rep')), may hold values from -6 to 6
- tiles: bfloat16 [512, 8, 128, 128], P(('row', 'rep')), may hold values from -0.1875 to 0.1875
- columns: int32 [512, 8], P(('row', 'rep')), may hold values from 0 to 511, as said below
- w_aggregate: bfloat16 [512, 512], replicated, may hold values from -0.25 to 0.25
- w_self: bfloat16 [512, 512], replicated, may hold values from -0.25 to 0.25
- w_middle: bfloat16 [512, 512], replicated, may hold values from -0.25 to 0.25
- w_output: bfloat16 [512, 512], replicated, may hold values from -0.25 to 0.25
- cotangent: bfloat16 [65536, 512], P(('row', 'rep')), may hold values from -6 to 6
Outputs:
- updated: bfloat16 [65536, 512], P(('row', 'rep'))
- grad_features: bfloat16 [65536, 512], P(('row', 'rep'))
- grad_output: float32 [512, 512], P('rep')
- grad_middle: float32 [512, 512], P('rep')
- grad_aggregate: float32 [512, 512], P('rep')
- grad_self: float32 [512, 512], P('rep')
Inputs may be any that keep to these rules, and one draw needn't show every extreme that they name: `columns`: row group g holds row blocks g * 32 to (g + 1) * 32 - 1, for g < 16. Every column block named by a row block of group g lies in group g - 1, g or g + 1, taken modulo 16; every row block names each of these three groups at least once. Column blocks may repeat within a row block.
All inputs are finite; a program needn't handle non-finite values.
Results may differ from a plain program's by a relative error of at most 0.015.
Values may be sent and summed in bfloat16 or wider, within the bound.
A program may use at most 192 MiB of HBM per device.

v0:
```python
import math

import jax
import jax.numpy as jnp
from jax import lax
from jax.sharding import PartitionSpec as P


def from_behind(value, axis, steps):
    count = lax.axis_size(axis)
    pairs = [(source, (source + steps) % count) for source in range(count)]
    return lax.ppermute(value, axis, pairs)


def silu_slope(value):
    sig = jax.nn.sigmoid(value)
    return sig * (1.0 + value * (1.0 - sig))


def times_transposed(left_operand, weight):
    return lax.dot_general(
        left_operand, weight, (((1,), (1,)), ((), ())), preferred_element_type=jnp.float32
    )


def local(features, tiles, columns, w_aggregate, w_self, w_middle, w_output, cotangent):
    blocks_dev, width_k, tile_size, _ = tiles.shape
    width = features.shape[1]
    groups = lax.axis_size("row")
    replicas = lax.axis_size("rep")
    panel_blocks = replicas * blocks_dev
    panel_rows = panel_blocks * tile_size
    group_id = lax.axis_index("row")
    slot_of = (columns // panel_blocks - group_id + 1) % groups
    window_index = slot_of * panel_blocks + columns % panel_blocks
    own_panel = lax.all_gather(features, "rep", axis=0, tiled=True)
    prior_panel = from_behind(own_panel, "row", 1)
    next_panel = from_behind(own_panel, "row", -1)
    window = jnp.concatenate([prior_panel, own_panel, next_panel], 0).reshape(
        3 * panel_blocks, tile_size, width
    )
    picked = window[window_index]
    summed = jnp.einsum("bkij,bkjf->bif", tiles, picked, preferred_element_type=jnp.float32)
    aggregate = summed.reshape(blocks_dev * tile_size, width).astype(jnp.bfloat16)
    pre_first = jnp.dot(aggregate, w_aggregate, preferred_element_type=jnp.float32) + jnp.dot(
        features, w_self, preferred_element_type=jnp.float32
    )
    first = jax.nn.silu(pre_first).astype(jnp.bfloat16)
    pre_second = jnp.dot(first, w_middle, preferred_element_type=jnp.float32)
    second = jax.nn.silu(pre_second).astype(jnp.bfloat16)
    updated = (
        features.astype(jnp.float32) + jnp.dot(second, w_output, preferred_element_type=jnp.float32)
    ).astype(jnp.bfloat16)
    delta_second = (times_transposed(cotangent, w_output) * silu_slope(pre_second)).astype(
        jnp.bfloat16
    )
    delta_first = (times_transposed(delta_second, w_middle) * silu_slope(pre_first)).astype(
        jnp.bfloat16
    )
    delta_aggregate = times_transposed(delta_first, w_aggregate).astype(jnp.bfloat16)
    delta_blocks = delta_aggregate.reshape(blocks_dev, tile_size, width)
    messages = jnp.einsum("bkji,bjf->bkif", tiles, delta_blocks, preferred_element_type=jnp.float32)
    spread = jnp.zeros((3 * panel_blocks, tile_size, width), jnp.float32)
    spread = spread.at[window_index.reshape(-1)].add(messages.reshape(-1, tile_size, width))
    spread = spread.reshape(3 * panel_rows, width)
    prior_part = spread[:panel_rows]
    own_part = spread[panel_rows : 2 * panel_rows]
    next_part = spread[2 * panel_rows :]
    from_next = from_behind(prior_part.astype(jnp.bfloat16), "row", -1).astype(prior_part.dtype)
    from_prior = from_behind(next_part.astype(jnp.bfloat16), "row", 1).astype(next_part.dtype)
    returned = lax.psum_scatter(
        (own_part + from_next + from_prior).astype(jnp.bfloat16),
        "rep",
        scatter_dimension=0,
        tiled=True,
    ).astype(jnp.float32)
    grad_features = (
        cotangent.astype(jnp.float32) + times_transposed(delta_first, w_self) + returned
    ).astype(jnp.bfloat16)
    total_nodes = features.shape[0] * groups * replicas
    scale = 1.0 / math.sqrt(total_nodes)
    local_output = jnp.dot(second.T, cotangent, preferred_element_type=jnp.float32)
    local_middle = jnp.dot(first.T, delta_second, preferred_element_type=jnp.float32)
    local_aggregate = jnp.dot(aggregate.T, delta_first, preferred_element_type=jnp.float32)
    local_self = jnp.dot(features.T, delta_first, preferred_element_type=jnp.float32)
    share_rows = width // replicas
    totals = lax.psum((local_output, local_middle, local_aggregate, local_self), ("row", "rep"))
    start_row = lax.axis_index("rep") * share_rows
    totals = tuple(
        (lax.dynamic_slice_in_dim(member, start_row, share_rows, 0) for member in totals)
    )
    return (
        updated,
        grad_features,
        totals[0] * scale,
        totals[1] * scale,
        totals[2] * scale,
        totals[3] * scale,
    )


def solution(mesh):
    placed = (
        P(("row", "rep"), None),
        P(("row", "rep"), None, None, None),
        P(("row", "rep"), None),
        P(),
        P(),
        P(),
        P(),
        P(("row", "rep"), None),
    )
    return jax.shard_map(
        local,
        mesh=mesh,
        in_specs=placed,
        out_specs=(
            P(("row", "rep"), None),
            P(("row", "rep"), None),
            P("rep", None),
            P("rep", None),
            P("rep", None),
            P("rep", None),
        ),
        check_vma=False,
    )
```

profile of v0, /device:TPU:1, one launch (start us, length us, event | category | flops | bytes accessed | tf_op | source)
XLA Modules:
  0.0 566.3 jit_solution(3026869364455568108)
XLA Ops:
  8.0 73.7 %all-gather.2.cloned.1.call-done = bf16[4096,512]{1,0:T(8,128)(2,1)} async-done(((bf16[256,512]{1,0:T(8,128)(2,1)}), bf16[4096,512]{1,0:T(8,128)(2,1)}) %all-gather.2.cloned.1.call-update) | async-done | bytes 4194320 | tf_op jit(solution)/shard_map/all_gather | solution.py:36
  81.7 9.5 %collective-permute-start.1 = (bf16[4096,512]{1,0:T(8,128)(2,1)}, bf16[4096,512]{1,0:T(8,128)(2,1)}, u32[]{:S(2)}, u32[]{:S(2)}) collective-permute-start(bf16[4096,512]{1,0:T(8,128)(2,1)} %all-gather.2.cloned.1.call-done), channel_id=1, source_target_pairs={{0,240},{16,0},{32,16},{48,32},{64,48},{80,64},{96,80},{112,96},{1... | collective-permute-start | bytes 12582920 | tf_op jit(solution)/shard_map/ppermute | solution.py:12
  91.2 1.1 collective-permute-start
  92.2 0.7 compare_select_fusion
  93.1 45.9 %collective-permute-done.1 = bf16[4096,512]{1,0:T(8,128)(2,1)} collective-permute-done((bf16[4096,512]{1,0:T(8,128)(2,1)}, bf16[4096,512]{1,0:T(8,128)(2,1)}, u32[]{:S(2)}, u32[]{:S(2)}) %collective-permute-start.1) | collective-permute-done | bytes 4194336 | tf_op jit(solution)/shard_map/ppermute | solution.py:12
  139.0 15.9 %pad_maximum_fusion = bf16[12288,512]{1,0:T(8,128)(2,1)} fusion(bf16[4096,512]{1,0:T(8,128)(2,1)} %collective-permute-done.1, bf16[4096,512]{1,0:T(8,128)(2,1)} %all-gather.2.cloned.1.call-done, bf16[4096,512]{1,0:T(8,128)(2,1)} %collective-permute-done), kind=kLoop, calls=%fused_computation.2 | loop fusion | flops 37748736 | bytes 25165824 | tf_op jit(solution)/shard_map/concatenate | solution.py:39
  155.0 5.3 gather_fusion
  160.8 1.4 fusion.15
  163.3 0.7 copy-done.10
  164.7 2.7 fusion.16
  167.4 5.4 copy.15
  172.8 11.5 %broadcast_in_dim.8 = f32[96,128,512]{2,1,0:T(8,128)} broadcast(f32[]{:T(128)} %constant.62.clone.1), dimensions={} | broadcast | bytes 25165828 | tf_op jit(solution)/shard_map/broadcast_in_dim | solution.py:63
  184.3 9.6 %scatter_fusion = f32[96,128,512]{2,1,0:T(8,128)} fusion(f32[96,128,512]{2,1,0:T(8,128)} %broadcast_in_dim.8, s32[16]{0:T(128)S(1)} %fusion.9, f32[16,128,512]{2,1,0:T(8,128)} %copy.15), kind=kCustom, calls=%fused_computation.1 | custom fusion | flops 1048576 | bytes 12582976 | tf_op jit(solution)/shard_map/scatter-add | solution.py:64
  193.9 9.3 %convert.4 = bf16[96,128,512]{2,1,0:T(8,128)(2,1)S(1)} convert(f32[96,128,512]{2,1,0:T(8,128)} %scatter_fusion) | non-fusion elementwise | flops 6291456 | bytes 37748736 | tf_op jit(solution)/shard_map/convert.1
  203.2 3.5 fusion.14
  206.7 1.5 collective-permute-start.3
  208.3 2.5 collective-permute-start.2
  210.8 1.3 fusion.17
  212.1 1.4 convolution_bitcast_fusion
  213.5 1.3 fusion.11
  214.8 1.4 fusion.10
  216.3 8.2 %slice.22 = f32[32,128,512]{2,1,0:T(8,128)} slice(f32[96,128,512]{2,1,0:T(8,128)} %scatter_fusion), slice={[32:64], [0:128], [0:512]} | slice | bytes 16777216 | tf_op jit(solution)/shard_map/slice | solution.py:67
  224.5 32.6 %collective-permute-done.3 = bf16[4096,512]{1,0:T(8,128)(2,1)} collective-permute-done((bf16[4096,512]{1,0:T(8,128)(2,1)}, bf16[4096,512]{1,0:T(8,128)(2,1)}, u32[]{:S(2)}, u32[]{:S(2)}) %collective-permute-start.3) | collective-permute-done | bytes 4194336 | tf_op jit(solution)/shard_map/ppermute | solution.py:12
  257.1 3.4 collective-permute-done.2
  260.5 9.7 %fusion.1 = bf16[4096,512]{1,0:T(8,128)(2,1)} fusion(f32[32,128,512]{2,1,0:T(8,128)} %slice.22, bf16[4096,512]{1,0:T(8,128)(2,1)} %collective-permute-done.3, bf16[4096,512]{1,0:T(8,128)(2,1)} %collective-permute-done.2), kind=kLoop, calls=%fused_computation.5 | loop fusion | flops 10485760 | bytes 20971520 | tf_op jit(solution)/shard_map/convert_element_type | solution.py:72
  270.2 1.0 copy-done.9
  271.2 1.0 fusion.3
  272.6 213.5 %all-reduce.3.cloned.1.call-done = (f32[512,512]{1,0:T(8,128)}, f32[512,512]{1,0:T(8,128)}, f32[512,512]{1,0:T(8,128)}, f32[512,512]{1,0:T(8,128)}) async-done(((f32[512,512]{1,0:T(8,128)}, f32[512,512]{1,0:T(8,128)}, f32[512,512]{1,0:T(8,128)}, f32[512,512]{1,0:T(8,128)}), (f32[512,512]{1,0:T(8,128)}, f32[512,512]{1,0:T(8,128)}, f32[512,512]{1,0:T(8,128)}, ...) | async-done | bytes 4194320 | tf_op jit(solution)/shard_map/psum | solution.py:87
  486.0 1.5 dynamic-slice_multiply_fusion.2
  487.6 1.5 dynamic-slice_multiply_fusion
  489.1 69.0 %reduce-scatter.2.cloned.1.call-done = bf16[256,512]{1,0:T(8,128)(2,1)} async-done(((bf16[4096,512]{1,0:T(8,128)(2,1)}), bf16[256,512]{1,0:T(8,128)(2,1)}) %reduce-scatter.2.cloned.1.call-update) | async-done | bytes 262160 | tf_op jit(solution)/shard_map/reduce_scatter | solution.py:71
  558.1 1.7 add_convert_fusion
  (40 shorter events, 3.6 us)
Async XLA Ops:
  7.2 153.1 %copy-start = (bf16[2,8,128,128]{3,2,1,0:T(8,128)(2,1)S(1)}, bf16[2,8,128,128]{3,2,1,0:T(8,128)(2,1)}, u32[]{:S(2)}) copy-start(bf16[2,8,128,128]{3,2,1,0:T(8,128)(2,1)} %param.9) | copy-start | bytes 1572868
  7.2 74.5 %all-gather.2.cloned.1.call-start = ((), (), s32[]{:S(2)}) async-start(), calls=%async_computation.1 | async-start | bytes 4456448 | tf_op jit(solution)/shard_map/all_gather | solution.py:36
  7.9 478.1 %all-reduce.3.cloned.1.call-start = ((), (), s32[]{:S(2)}) async-start(), calls=%async_computation.3 | async-start | bytes 8388608 | tf_op jit(solution)/shard_map/psum | solution.py:87
  81.7 57.4 %collective-permute-start.1 = (bf16[4096,512]{1,0:T(8,128)(2,1)}, bf16[4096,512]{1,0:T(8,128)(2,1)}, u32[]{:S(2)}, u32[]{:S(2)}) collective-permute-start(bf16[4096,512]{1,0:T(8,128)(2,1)} %all-gather.2.cloned.1.call-done), channel_id=1, source_target_pairs={{0,240},{16,0},{32,16},{48,32},{64,48},{80,64},{96,80},{112,96},{1... | collective-permute-start | bytes 12582920 | tf_op jit(solution)/shard_map/ppermute | solution.py:12
  91.2 47.9 %collective-permute-start = (bf16[4096,512]{1,0:T(8,128)(2,1)}, bf16[4096,512]{1,0:T(8,128)(2,1)}, u32[]{:S(2)}, u32[]{:S(2)}) collective-permute-start(bf16[4096,512]{1,0:T(8,128)(2,1)} %all-gather.2.cloned.1.call-done), channel_id=1, source_target_pairs={{0,16},{16,32},{32,48},{48,64},{64,80},{80,96},{96,112},{112,128},... | collective-permute-start | bytes 12582920 | tf_op jit(solution)/shard_map/ppermute | solution.py:12
  155.0 7.2 %copy-start.2 = (bf16[256,512]{1,0:T(8,128)(2,1)S(1)}, bf16[256,512]{1,0:T(8,128)(2,1)}, u32[]{:S(2)}) copy-start(bf16[256,512]{1,0:T(8,128)(2,1)} %param.8) | copy-start | bytes 786436
  160.3 1.9 copy-start.3
  160.3 2.2 copy-start.7
  160.3 2.5 copy-start.6
  160.3 2.5 copy-start.8
  162.9 1.5 copy-start.5
  163.3 0.7 copy-start.10
  203.2 10.3 %copy-start.11 = (bf16[256,512]{1,0:T(8,128)(2,1)S(1)}, bf16[256,512]{1,0:T(8,128)(2,1)}, u32[]{:S(2)}) copy-start(bf16[256,512]{1,0:T(8,128)(2,1)} %copy-done.10) | copy-start | bytes 786436
  206.7 50.3 %collective-permute-start.3 = (bf16[4096,512]{1,0:T(8,128)(2,1)}, bf16[4096,512]{1,0:T(8,128)(2,1)}, u32[]{:S(2)}, u32[]{:S(2)}) collective-permute-start(bf16[4096,512]{1,0:T(8,128)(2,1)} %bitcast.13), channel_id=1, source_target_pairs={{0,16},{16,32},{32,48},{48,64},{64,80},{80,96},{96,112},{112,128},... | collective-permute-start | bytes 12582920 | tf_op jit(solution)/shard_map/ppermute | solution.py:12
  208.3 52.2 %collective-permute-start.2 = (bf16[4096,512]{1,0:T(8,128)(2,1)}, bf16[4096,512]{1,0:T(8,128)(2,1)}, u32[]{:S(2)}, u32[]{:S(2)}) collective-permute-start(bf16[4096,512]{1,0:T(8,128)(2,1)} %bitcast.12), channel_id=1, source_target_pairs={{0,240},{16,0},{32,16},{48,32},{64,48},{80,64},{96,80},{112,96},{1... | collective-permute-start | bytes 12582920 | tf_op jit(solution)/shard_map/ppermute | solution.py:12
  216.2 341.8 %reduce-scatter.2.cloned.1.call-start = ((), (), s32[]{:S(2)}) async-start(), calls=%async_computation.2 | async-start | bytes 4456448 | tf_op jit(solution)/shard_map/reduce_scatter | solution.py:71
  270.1 1.0 copy-start.9
  270.1 2.1 copy-start.4
  270.2 289.6 %copy-start.1 = (bf16[2,8,128,128]{3,2,1,0:T(8,128)(2,1)S(1)}, bf16[2,8,128,128]{3,2,1,0:T(8,128)(2,1)}, u32[]{:S(2)}) copy-start(bf16[2,8,128,128]{3,2,1,0:T(8,128)(2,1)} %param.9) | copy-start | bytes 1572868
Sparse Core Ops, SparseCore 0:
  9.8 71.8 all-gather.1
  216.4 269.6 all-reduce.2
  488.8 69.2 reduce-scatter.1
where the time goes:
time: 577 us; the launch traced here: 566 us
  waiting for transfers between devices  439 us (76%)
  other arithmetic  50 us (9%)
  local copies, waits for them, and re-layouts  35.9 us (6%)
  starting transfers between devices  14.7 us (3%)
  between operations  14 us (2%)
  matrix products  13 us (2%)
    psum x1, waiting for transfers between devices, local(): lax.psum((local_output, local_middle, local_aggregate, local_self), ('row...  213 us
    ppermute x4, waiting for transfers between devices, from_behind(): return lax.ppermute(value, axis, pairs)  81.9 us
    all_gather x1, waiting for transfers between devices, local(): own_panel = lax.all_gather(features, 'rep', axis=0, tiled=True)  73.7 us
    reduce_scatter x1, waiting for transfers between devices, local(): lax.psum_scatter((own_part + from_next + from_prior).astype(jnp.bfloat16)...  69 us
    concatenate x1, other arithmetic, local(): jnp.concatenate([prior_panel, own_panel, next_panel], 0)  15.9 us
    ppermute x4, starting transfers between devices, from_behind(): return lax.ppermute(value, axis, pairs)  14.6 us
  transfers between devices with their start and end apart: 7, of which 6 were waited for; matrix products, arithmetic and copies ran while one was open for 5% of the time, Pallas kernels for 0%

commit v1 on v0

v1 whole, which is shorter than its diff:
```python
import math

import jax
import jax.numpy as jnp
from jax import lax
from jax.experimental import pallas as pl
from jax.experimental.pallas import tpu as pltpu
from jax.sharding import PartitionSpec as P

MESH = pl.DeviceIdType.MESH
BF = jnp.bfloat16
F32 = jnp.float32
VMEM = pltpu.VMEM
DMA = pltpu.SemaphoreType.DMA


def wrap16(value):
    return lax.rem(value + 16, 16)


def quarter(rep):
    return (rep // 8) * 2 + rep % 2


def mate(rep, core, part):
    z = rep % 8
    step = jnp.where((z + core) % 2 == 0, 1, 7)
    other = (z + step) % 8
    return (part // 2) * 8 + jnp.where(z % 2 == part % 2, z, other)


def lanes(part, size=128):
    return pl.ds(pl.multiple_of(part * size, size), size)


def remote(src, dst, send, recv, row, rep):
    return pltpu.make_async_remote_copy(
        src_ref=src, dst_ref=dst, send_sem=send, recv_sem=recv, device_id=(row, rep), device_id_type=MESH
    )


def window_index(column, group):
    panel = jnp.minimum(lax.rem(lax.div(column, 32) - group + 17, 16), 2)
    return panel * 32 + lax.rem(column, 32)


def dot(a, b):
    return jnp.dot(a, b, preferred_element_type=F32)


def dot_bt(a, b):
    return lax.dot_general(a, b, (((1,), (1,)), ((), ())), preferred_element_type=F32)


def dot_at(a, b):
    return lax.dot_general(a, b, (((0,), (0,)), ((), ())), preferred_element_type=F32)


def silu_slope(value):
    sig = jax.nn.sigmoid(value)
    return sig * (1.0 + value * (1.0 - sig))


def greet(peers):
    barrier = pltpu.get_barrier_semaphore()
    for row, rep in peers:
        pl.semaphore_signal(barrier, inc=1, device_id=(row, rep), device_id_type=MESH)
    pl.semaphore_wait(barrier, len(peers))


def forward_kernel(
    feat, tiles, cols, w_agg, w_self, w_mid, w_out, cot,
    upd, base, tiles_t, cols_t, delt, grads,
    win, cols_s, aggq, aggr, dagg, self_part, cot_part,
    loc, s1, r1, sx, rx, st, rt, sc, rc, sa, ra, sd, rd,
):
    g = lax.axis_index("row")
    r = lax.axis_index("rep")
    core = g % 2
    f = quarter(r)
    up, down = wrap16(g + 1), wrap16(g - 1)
    greet([(g, wrap16(r + o)) for o in range(1, 16)] + [(up, r), (down, r)])

    def slot(panel, rep):
        return win.at[pl.ds(panel * 32 + rep * 2, 2)]

    def plane_copy(o):
        peer = wrap16(r + o)
        return remote(
            feat.at[:, :, lanes(quarter(peer))], slot(1, r), s1.at[o], r1.at[o], g, peer
        )

    def plane_arrival(o):
        src = wrap16(r - o)
        return remote(slot(1, src), slot(1, src), s1.at[o], r1.at[o], g, src)

    def ring_copies(o):
        src = wrap16(r - o)
        return (
            remote(slot(1, src), slot(0, src), sx.at[0, o], rx.at[0, o], up, r),
            remote(slot(1, src), slot(2, src), sx.at[1, o], rx.at[1, o], down, r),
        )

    def ring_arrivals(o):
        src = wrap16(r - o)
        return (
            remote(slot(0, src), slot(0, src), sx.at[0, o], rx.at[0, o], down, r),
            remote(slot(2, src), slot(2, src), sx.at[1, o], rx.at[1, o], up, r),
        )

    def team(j):
        part = (f + j) % 4
        return part, mate(r, core, part)

    own = pltpu.make_async_copy(feat.at[:, :, lanes(f)], slot(1, r), loc.at[0])
    own.start()
    own_tiles = pltpu.make_async_copy(tiles, tiles_t.at[pl.ds(f * 16, 16)], loc.at[1])
    own_tiles.start()
    own_cols = pltpu.make_async_copy(cols, cols_t.at[f], loc.at[2])
    own_cols.start()

    @pl.loop(1, 16)
    def _(o):
        plane_copy(o).start()

    def tile_copy(j):
        peer = team(j)[1]
        return (
            remote(cols, cols_t.at[f], sc.at[j], rc.at[j], g, peer),
            remote(tiles, tiles_t.at[pl.ds(f * 16, 16)], st.at[j], rt.at[j], g, peer),
        )

    def tile_arrival(j):
        part, peer = team(4 - j)
        return (
            remote(cols_t.at[part], cols_t.at[part], sc.at[j], rc.at[j], g, peer),
            remote(
                tiles_t.at[pl.ds(part * 16, 16)], tiles_t.at[pl.ds(part * 16, 16)], st.at[j], rt.at[j], g, peer
            ),
        )

    for j in range(1, 4):
        for copy in tile_copy(j):
            copy.start()
    own.wait()
    for copy in ring_copies(0):
        copy.start()

    feat2 = feat[...].reshape(256, 512)
    cot2 = cot[...]
    self_part[...] = dot(feat2, w_self[...])
    cot_part[...] = dot_bt(cot2, w_out[...])

    @pl.loop(1, 16)
    def _(o):
        plane_arrival(o).wait_recv()
        for copy in ring_copies(o):
            copy.start()

    own_cols.wait()
    for j in range(1, 4):
        tile_arrival(j)[0].wait_recv()
    to_smem = pltpu.make_async_copy(cols_t, cols_s, loc.at[3])
    to_smem.start()
    to_smem.wait()
    own_tiles.wait()
    for j in range(1, 4):
        tile_arrival(j)[1].wait_recv()

    @pl.loop(0, 16)
    def _(o):
        for copy in ring_arrivals(o):
            copy.wait_recv()

    def agg_copy(j):
        part, peer = team(j)
        return remote(
            aggq.at[pl.ds(part * 2, 2)], aggr.at[:, :, lanes(f)], sa.at[j], ra.at[j], g, peer
        )

    def agg_arrival(j):
        part, peer = team(4 - j)
        view = aggr.at[:, :, lanes(part)]
        return remote(view, view, sa.at[j], ra.at[j], g, peer)

    def block_sum(part, half):
        picked = []
        for k in range(8):
            c = cols_s[part, half, k]
            index = window_index(c, g)
            picked.append(win[index])
        left = jnp.concatenate([tiles_t[part * 16 + half * 8 + k] for k in range(8)], axis=1)
        return dot(left, jnp.concatenate(picked, axis=0)).astype(BF)

    for j in (1, 2, 3, 0):
        part, peer = team(j)
        for half in range(2):
            total = block_sum(part, half)
            if j:
                aggq[part * 2 + half] = total
            else:
                aggr[half, :, lanes(f)] = total
        if j:
            agg_copy(j).start()
    for j in range(1, 4):
        agg_arrival(j).wait_recv()

    agg = aggr[...].reshape(256, 512)
    pre_first = dot(agg, w_agg[...]) + self_part[...]
    first = (pre_first * jax.nn.sigmoid(pre_first)).astype(BF)
    pre_second = dot(first, w_mid[...])
    second = (pre_second * jax.nn.sigmoid(pre_second)).astype(BF)
    delta_second = (cot_part[...] * silu_slope(pre_second)).astype(BF)
    delta_first = (dot_bt(delta_second, w_mid[...]) * silu_slope(pre_first)).astype(BF)
    dagg[...] = dot_bt(delta_first, w_agg[...]).astype(BF).reshape(2, 128, 512)

    def delta_copy(j):
        part, peer = team(j)
        return remote(
            dagg.at[:, :, lanes(part)], delt.at[pl.ds(f * 2, 2)], sd.at[j], rd.at[j], g, peer
        )

    def delta_arrival(j):
        part, peer = team(4 - j)
        view = delt.at[pl.ds(part * 2, 2)]
        return remote(view, view, sd.at[j], rd.at[j], g, peer)

    for j in range(1, 4):
        delta_copy(j).start()
    delt[pl.ds(f * 2, 2)] = dagg[:, :, lanes(f)]
    upd[...] = (feat2.astype(F32) + dot(second, w_out[...])).astype(BF)
    base[...] = (cot2.astype(F32) + dot_bt(delta_first, w_self[...])).reshape(2, 128, 512)
    grads[0] = dot_at(second, cot2).astype(BF)
    grads[1] = dot_at(first, delta_second).astype(BF)
    grads[2] = dot_at(agg, delta_first).astype(BF)
    grads[3] = dot_at(feat2, delta_first).astype(BF)
    for j in range(1, 4):
        delta_arrival(j).wait_recv()

    @pl.loop(1, 16)
    def _(o):
        plane_copy(o).wait_send()

    @pl.loop(0, 16)
    def _(o):
        for copy in ring_copies(o):
            copy.wait_send()

    for j in range(1, 4):
        for copy in tile_copy(j):
            copy.wait_send()
        agg_copy(j).wait_send()
        delta_copy(j).wait_send()


def spread_kernel(cols_s, group, tiles_t, delt, out, acc):
    g = group[0]

    @pl.loop(0, 96)
    def _(i):
        acc[i] = jnp.zeros((128, 128), F32)

    @pl.loop(0, 8)
    def _(i):
        delta = delt[i]
        for k in range(8):
            c = cols_s[i * 8 + k]
            index = window_index(c, g)
            acc[index] += dot_at(tiles_t[i * 8 + k], delta)

    @pl.loop(0, 96)
    def _(i):
        out[i] = acc[i].astype(BF)


def return_kernel(
    scale,
    msgs, base, grads,
    gf, gout,
    from_prior, from_next, sums, parts, half_in, half, ring_in, ring, pair_in, pair, rep_in, piece,
    sx, rx, sp, rp, s_core, r_core, s_ring, r_ring, s_pair, r_pair, s_rep, r_rep, s_row, r_row,
):
    g = lax.axis_index("row")
    r = lax.axis_index("rep")
    core = g % 2
    x = (g // 2) % 4
    y_hi = g // 8
    up, down = wrap16(g + 1), wrap16(g - 1)
    sibling = g + 1 - 2 * core
    across = (g + 8) % 16
    greet([(g, wrap16(r + o)) for o in range(1, 16)] + [(wrap16(g + o), r) for o in range(1, 16)])

    def pick(panel, rep):
        return msgs.at[pl.ds(panel * 32 + rep * 2, 2)]

    def ring_copies(o):
        s = wrap16(r + o)
        return (
            remote(pick(0, s), from_next.at[pl.ds(s * 2, 2)], sx.at[0, o], rx.at[0, o], down, r),
            remote(pick(2, s), from_prior.at[pl.ds(s * 2, 2)], sx.at[1, o], rx.at[1, o], up, r),
        )

    def ring_arrivals(o):
        s = wrap16(r + o)
        a = from_next.at[pl.ds(s * 2, 2)]
        b = from_prior.at[pl.ds(s * 2, 2)]
        return (
            remote(a, a, sx.at[0, o], rx.at[0, o], up, r),
            remote(b, b, sx.at[1, o], rx.at[1, o], down, r),
        )

    core_copy = remote(grads.at[:, :, lanes(1 - core, 256)], half_in, s_core, r_core, sibling, r)
    core_copy.start()

    @pl.loop(0, 16)
    def _(i):
        for copy in ring_copies(lax.rem(i + 1, 16)):
            copy.start()

    core_copy.wait_recv()
    for m in range(4):
        half[m] = (grads[m, :, lanes(core, 256)].astype(F32) + half_in[m].astype(F32)).astype(BF)

    def x_row(j):
        return y_hi * 8 + ((x + j) % 4) * 2 + core

    def x_copy(j):
        return remote(half.at[(x + j) % 4], ring_in.at[j - 1], s_ring.at[j], r_ring.at[j], x_row(j), r)

    for j in range(1, 4):
        x_copy(j).start()

    def plane_copy(o):
        s = wrap16(r + o)
        return remote(sums.at[pl.ds(s * 2, 2)], parts.at[pl.ds(r * 2, 2)], sp.at[o], rp.at[o], g, s)

    def plane_arrival(o):
        s = wrap16(r - o)
        view = parts.at[pl.ds(s * 2, 2)]
        return remote(view, view, sp.at[o], rp.at[o], g, s)

    def total(s):
        return (
            msgs[pl.ds(32 + s * 2, 2)].astype(F32)
            + from_next[pl.ds(s * 2, 2)].astype(F32)
            + from_prior[pl.ds(s * 2, 2)].astype(F32)
        ).astype(BF)

    @pl.loop(1, 16)
    def _(o):
        for copy in ring_arrivals(o):
            copy.wait_recv()
        s = wrap16(r + o)
        sums[pl.ds(s * 2, 2)] = total(s)
        plane_copy(o).start()

    for copy in ring_arrivals(0):
        copy.wait_recv()
    parts[pl.ds(r * 2, 2)] = total(r)

    for j in range(1, 4):
        x_copy(j).wait_recv()
    ring[...] = (
        half[x].astype(F32) + ring_in[0].astype(F32) + ring_in[1].astype(F32) + ring_in[2].astype(F32)
    ).astype(BF)
    pair_copy = remote(ring.at[:, lanes(1 - y_hi)], pair_in, s_pair, r_pair, across, r)
    pair_copy.start()
    pair_copy.wait_recv()
    pair[...] = (ring[:, lanes(y_hi)].astype(F32) + pair_in[...].astype(F32)).astype(BF)

    def rep_copy(o):
        s = wrap16(r + o)
        rows = pl.ds(pl.multiple_of(s * 32, 32), 32)
        return remote(pair.at[rows], rep_in.at[o], s_rep.at[o], r_rep.at[o], g, s)

    @pl.loop(1, 16)
    def _(o):
        rep_copy(o).start()

    rep_in[0] = pair[pl.ds(pl.multiple_of(r * 32, 32), 32)]

    @pl.loop(1, 16)
    def _(o):
        plane_arrival(o).wait_recv()

    for f in range(4):
        cut = slice(f * 128, f * 128 + 128)
        value = base[:, :, cut]
        for t in range(4):
            s = (f // 2) * 8 + 2 * t + f % 2
            value = value + parts[2 * s : 2 * s + 2].astype(F32)
        gf[:, :, cut] = value.astype(BF)

    @pl.loop(1, 16)
    def _(o):
        rep_copy(o).wait_recv()

    acc = rep_in[0].astype(F32)
    for o in range(1, 16):
        acc = acc + rep_in[o].astype(F32)
    piece[...] = acc * scale

    def place(row):
        return gout.at[(row // 2) % 4, :, lanes((row % 2) * 2 + row // 8)]

    def row_copy(o):
        return remote(piece, place(g), s_row.at[o], r_row.at[o], wrap16(g + o), r)

    def row_arrival(o):
        src = wrap16(g - o)
        return remote(piece, place(src), s_row.at[o], r_row.at[o], src, r)

    @pl.loop(1, 16)
    def _(o):
        row_copy(o).start()

    gout[x, :, lanes(core * 2 + y_hi)] = piece[...]

    @pl.loop(1, 16)
    def _(o):
        row_arrival(o).wait_recv()

    @pl.loop(0, 16)
    def _(o):
        for copy in ring_copies(o):
            copy.wait_send()

    @pl.loop(1, 16)
    def _(o):
        plane_copy(o).wait_send()
        rep_copy(o).wait_send()
        row_copy(o).wait_send()

    core_copy.wait_send()
    pair_copy.wait_send()
    for j in range(1, 4):
        x_copy(j).wait_send()


def shape(dims, kind):
    return jax.ShapeDtypeStruct(dims, kind)


def local(features, tiles, columns, w_aggregate, w_self, w_middle, w_output, cotangent):
    vmem = pl.BlockSpec(memory_space=VMEM)
    smem = pl.BlockSpec(memory_space=pltpu.SMEM)
    limit = 52 * 1024 * 1024
    feat = features.reshape(2, 128, 512)
    upd, base, tiles_t, cols_t, delt, grads = pl.pallas_call(
        forward_kernel,
        out_shape=(
            shape((256, 512), BF),
            shape((2, 128, 512), F32),
            shape((64, 128, 128), BF),
            shape((4, 2, 8), jnp.int32),
            shape((8, 128, 128), BF),
            shape((4, 512, 512), BF),
        ),
        in_specs=[vmem] * 8,
        out_specs=[vmem] * 6,
        scratch_shapes=[
            VMEM((96, 128, 128), BF),
            pltpu.SMEM((4, 2, 8), jnp.int32),
            VMEM((8, 128, 128), BF),
            VMEM((2, 128, 512), BF),
            VMEM((2, 128, 512), BF),
            VMEM((256, 512), F32),
            VMEM((256, 512), F32),
            DMA((4,)),
            DMA((16,)), DMA((16,)),
            DMA((2, 16)), DMA((2, 16)),
            DMA((4,)), DMA((4,)),
            DMA((4,)), DMA((4,)),
            DMA((4,)), DMA((4,)),
            DMA((4,)), DMA((4,)),
        ],
        compiler_params=pltpu.CompilerParams(
            collective_id=0, has_side_effects=True, vmem_limit_bytes=limit
        ),
        name="forward_pass",
    )(feat, tiles.reshape(16, 128, 128), columns, w_aggregate, w_self, w_middle, w_output, cotangent)
    group = lax.axis_index("row").astype(jnp.int32).reshape(1)
    msgs = pl.pallas_call(
        spread_kernel,
        out_shape=shape((96, 128, 128), BF),
        in_specs=[smem, smem, vmem, vmem],
        out_specs=vmem,
        scratch_shapes=[VMEM((96, 128, 128), F32)],
        compiler_params=pltpu.CompilerParams(vmem_limit_bytes=limit),
        name="spread_messages",
    )(cols_t.reshape(64), group, tiles_t, delt)
    scale = 1.0 / math.sqrt(features.shape[0] * lax.axis_size("row") * lax.axis_size("rep"))
    gf, gout = pl.pallas_call(
        lambda *refs: return_kernel(scale, *refs),
        out_shape=(shape((2, 128, 512), BF), shape((4, 32, 512), F32)),
        in_specs=[vmem] * 3,
        out_specs=[vmem] * 2,
        scratch_shapes=[
            VMEM((32, 128, 128), BF),
            VMEM((32, 128, 128), BF),
            VMEM((32, 128, 128), BF),
            VMEM((32, 128, 128), BF),
            VMEM((4, 512, 256), BF),
            VMEM((4, 512, 256), BF),
            VMEM((3, 512, 256), BF),
            VMEM((512, 256), BF),
            VMEM((512, 128), BF),
            VMEM((512, 128), BF),
            VMEM((16, 32, 128), BF),
            VMEM((32, 128), F32),
            DMA((2, 16)), DMA((2, 16)),
            DMA((16,)), DMA((16,)),
            DMA, DMA,
            DMA((4,)), DMA((4,)),
            DMA, DMA,
            DMA((16,)), DMA((16,)),
            DMA((16,)), DMA((16,)),
        ],
        compiler_params=pltpu.CompilerParams(
            collective_id=1, has_side_effects=True, vmem_limit_bytes=limit
        ),
        name="return_messages",
    )(msgs, base, grads)
    return upd, gf.reshape(256, 512), gout[0], gout[1], gout[2], gout[3]


def solution(mesh):
    placed = (
        P(("row", "rep"), None),
        P(("row", "rep"), None, None, None),
        P(("row", "rep"), None),
        P(),
        P(),
        P(),
        P(),
        P(("row", "rep"), None),
    )
    return jax.shard_map(
        local,
        mesh=mesh,
        in_specs=placed,
        out_specs=(
            P(("row", "rep"), None),
            P(("row", "rep"), None),
            P("rep", None),
            P("rep", None),
            P("rep", None),
            P("rep", None),
        ),
        check_vma=False,
    )
```

time: 577 us -> 139 us (0.24); the launches traced: 566 us -> 139 us
  waiting for transfers between devices: 439 us -> 0 us
  Pallas kernels: 0 us -> 133 us
  other arithmetic: 50 us -> 0 us
  local copies, waits for them, and re-layouts: 35.9 us -> 4.76 us
  starting transfers between devices: 14.7 us -> 0 us
  between operations: 14 us -> 0.67 us
  matrix products: 13 us -> 0 us
    psum x1 -> x0, waiting for transfers between devices: 213 us -> none  [local(): lax.psum((local_output, local_middle, local_aggregate, local_self), ('row...]
    pallas_call x0 -> x3, Pallas kernels: none -> 133 us  [the longest x1 70.8 us: local(): pl.pallas_call(forward_kernel, out_shape=(shape((256, 512), BF), shape((2...]
    ppermute x4 -> x0, waiting for transfers between devices: 81.9 us -> none  [from_behind(): return lax.ppermute(value, axis, pairs)]
    all_gather x1 -> x0, waiting for transfers between devices: 73.7 us -> none  [local(): own_panel = lax.all_gather(features, 'rep', axis=0, tiled=True)]
    reduce_scatter x1 -> x0, waiting for transfers between devices: 69 us -> none  [local(): lax.psum_scatter((own_part + from_next + from_prior).astype(jnp.bfloat16)...]
    concatenate x1 -> x0, other arithmetic: 15.9 us -> none  [local(): jnp.concatenate([prior_panel, own_panel, next_panel], 0)]
    ppermute x4 -> x0, starting transfers between devices: 14.6 us -> none  [from_behind(): return lax.ppermute(value, axis, pairs)]
    dot_general x14 -> x0, matrix products: 13 us -> none  [the longest x1 2.69 us: local(): jnp.einsum('bkji,bjf->bkif', tiles, delta_blocks, preferred_element_type=...]
  transfers between devices with their start and end apart: 7 -> 0, of which waited for: 6 -> 0; matrix products, arithmetic and copies ran while one was open for 5% -> 0% of each run, Pallas kernels for 0% -> 0%
where the time goes in v1:
time: 139 us
  Pallas kernels  133 us (96%)
  local copies, waits for them, and re-layouts  4.76 us (3%)
    pallas_call x1, Pallas kernels, local(): pl.pallas_call(forward_kernel, out_shape=(shape((256, 512), BF), shape((2...  70.8 us
    pallas_call x1, Pallas kernels, local(): pl.pallas_call(lambda *refs: return_kernel(scale, *refs), out_shape=(shap...  55.7 us
    pallas_call x1, Pallas kernels, local(): pl.pallas_call(spread_kernel, out_shape=shape((96, 128, 128), BF), in_spe...  6.78 us
    unnamed x8, local copies, waits for them, and re-layouts  3.98 us

profile of v1, /device:TPU:1, one launch (start us, length us, event | category | flops | bytes accessed | tf_op | source)
XLA Modules:
  0.0 138.7 jit_solution(18218790705730441611)
XLA Ops:
  0.6 0.0 copy-start
  0.6 0.9 copy-done
  1.6 0.0 copy-start.1
  1.6 0.9 copy-done.1
  2.5 0.0 copy-start.2
  2.5 0.7 copy-done.2
  3.2 70.8 %forward_pass.1 = (bf16[256,512]{1,0:T(8,128)(2,1)S(1)}, f32[2,128,512]{2,1,0:T(8,128)S(1)}, bf16[64,128,128]{2,1,0:T(8,128)(2,1)}, s32[4,2,8]{2,1,0:T(2,128)S(1...) custom-call(bf16[2,128,512]{2,1,0:T(8,128)(2,1)S(1)} %bitcast.12, bf16[16,128,128]{2,1,0:T(8,128)(2,1)} %bitcast.14, ...), custom_call_target="tpu_custom_call" | custom-call | tf_op jit(solution)/shard_map/forward_pass/pallas_call | solution.py:449
  74.0 0.1 reshape.29.cols_s
  74.1 6.8 %spread_messages.1.refs_0_ = bf16[96,128,128]{2,1,0:T(8,128)(2,1)} custom-call(s32[64]{0:T(128)S(1)} %reshape.29.cols_s, s32[1]{0:T(128)} %bitcast.2.group, bf16[64,128,128]{2,1,0:T(8,128)(2,1)} %get-tuple-element.16.tiles_t, bf16[8,128,128]{2,1,0:T(8,128)(2,1)S(1)} %get-tuple-element.17.delt), custom_call_target="tpu_custom_call" | custom-call | tf_op jit(solution)/shard_map/spread_messages/pallas_call | solution.py:483
  80.9 55.7 %return_messages.1 = (bf16[2,128,512]{2,1,0:T(8,128)(2,1)S(1)}, f32[4,32,512]{2,1,0:T(8,128)S(1)}) custom-call(bf16[96,128,128]{2,1,0:T(8,128)(2,1)} %spread_messages.1.refs_0_, f32[2,128,512]{2,1,0:T(8,128)S(1)} %get-tuple-element.18.refs_1_, bf16[4,512,512]{2,1,0:T(8,128)(2,1)} %get-tuple-element.19.refs_2_), custom_call_target="tpu_custom_call" | custom-call | tf_op jit(solution)/shard_map/return_messages/pallas_call | solution.py:493
  136.6 0.7 slice_bitcast_fusion
  137.3 0.7 copy.16
  138.0 0.7 copy.17
Async XLA Ops:
  0.6 1.0 copy-start
  1.6 0.9 copy-start.1
  2.5 0.7 copy-start.2

commit v2 on v1

v2 whole, which is shorter than its diff:
```python
import math

import jax
import jax.numpy as jnp
from jax import lax
from jax.experimental import pallas as pl
from jax.experimental.pallas import tpu as pltpu
from jax.sharding import PartitionSpec as P

MESH = pl.DeviceIdType.MESH
BF = jnp.bfloat16
F32 = jnp.float32
VMEM = pltpu.VMEM
DMA = pltpu.SemaphoreType.DMA


def wrap16(value):
    return lax.rem(value + 16, 16)


def quarter(rep):
    return (rep // 8) * 2 + rep % 2


def mate(rep, core, part):
    z = rep % 8
    step = jnp.where((z + core) % 2 == 0, 1, 7)
    other = (z + step) % 8
    return (part // 2) * 8 + jnp.where(z % 2 == part % 2, z, other)


def lanes(part, size=128):
    return pl.ds(pl.multiple_of(part * size, size), size)


def remote(src, dst, send, recv, row, rep):
    return pltpu.make_async_remote_copy(
        src_ref=src, dst_ref=dst, send_sem=send, recv_sem=recv, device_id=(row, rep), device_id_type=MESH
    )


def window_index(column, group):
    panel = jnp.minimum(lax.rem(lax.div(column, 32) - group + 17, 16), 2)
    return panel * 32 + lax.rem(column, 32)


def dot(a, b):
    return jnp.dot(a, b, preferred_element_type=F32)


def dot_bt(a, b):
    return lax.dot_general(a, b, (((1,), (1,)), ((), ())), preferred_element_type=F32)


def dot_at(a, b):
    return lax.dot_general(a, b, (((0,), (0,)), ((), ())), preferred_element_type=F32)


def silu_slope(value):
    sig = jax.nn.sigmoid(value)
    return sig * (1.0 + value * (1.0 - sig))


def greet(peers):
    barrier = pltpu.get_barrier_semaphore()
    for row, rep in peers:
        pl.semaphore_signal(barrier, inc=1, device_id=(row, rep), device_id_type=MESH)
    pl.semaphore_wait(barrier, len(peers))


def layer_kernel(
    scale,
    feat, tiles, cols, w_agg_h, w_self_h, w_mid_h, w_out_h, cot_h,
    upd, gf, gout,
    feat_v, cot_v, w_agg, w_self, w_mid, w_out,
    tiles_t, cols_t, win, cols_s, keys, table, table_s, aggq, aggr, dagg, delt, self_part, cot_part,
    base, grads, csum, to_next, to_prior, from_prior, from_next, sums, parts,
    half_in, half, ring_in, ring, pair_in, pair, rep_in, piece,
    loc, s1, r1, sx, rx, st, rt, sc, rc, sa, ra, sd, rd,
    sm, rm, sp, rp, s_core, r_core, s_ring, r_ring, s_pair, r_pair, s_rep, r_rep, s_row, r_row,
):
    g = lax.axis_index("row")
    r = lax.axis_index("rep")
    core = g % 2
    x = (g // 2) % 4
    y_hi = g // 8
    f = quarter(r)
    up, down = wrap16(g + 1), wrap16(g - 1)
    sibling = g + 1 - 2 * core
    across = (g + 8) % 16

    loads = [
        pltpu.make_async_copy(src, dst, loc.at[i])
        for i, (src, dst) in enumerate(
            (
                (feat, feat_v), (w_self_h, w_self), (cot_h, cot_v), (w_out_h, w_out),
                (w_agg_h, w_agg), (w_mid_h, w_mid),
                (tiles, tiles_t.at[pl.ds(f * 16, 16)]), (cols, cols_t.at[f]),
            )
        )
    ]
    for load in loads:
        load.start()
    greet([(g, wrap16(r + o)) for o in range(1, 16)] + [(wrap16(g + o), r) for o in range(1, 16)])

    def slot(panel, rep):
        return win.at[pl.ds(panel * 32 + rep * 2, 2)]

    def plane_copy(o):
        peer = wrap16(r + o)
        return remote(
            feat.at[:, :, lanes(quarter(peer))], slot(1, r), s1.at[o], r1.at[o], g, peer
        )

    def plane_arrival(o):
        src = wrap16(r - o)
        return remote(slot(1, src), slot(1, src), s1.at[o], r1.at[o], g, src)

    def ring_copies(o):
        src = wrap16(r - o)
        return (
            remote(slot(1, src), slot(0, src), sx.at[0, o], rx.at[0, o], up, r),
            remote(slot(1, src), slot(2, src), sx.at[1, o], rx.at[1, o], down, r),
        )

    def ring_arrivals(o):
        src = wrap16(r - o)
        return (
            remote(slot(0, src), slot(0, src), sx.at[0, o], rx.at[0, o], down, r),
            remote(slot(2, src), slot(2, src), sx.at[1, o], rx.at[1, o], up, r),
        )

    def team(j):
        part = (f + j) % 4
        return part, mate(r, core, part)

    def cols_copy(j):
        return remote(cols, cols_t.at[f], sc.at[j], rc.at[j], g, team(j)[1])

    def cols_arrival(j):
        part, peer = team(4 - j)
        return remote(cols_t.at[part], cols_t.at[part], sc.at[j], rc.at[j], g, peer)

    def tile_copy(j):
        return remote(tiles, tiles_t.at[pl.ds(f * 16, 16)], st.at[j], rt.at[j], g, team(j)[1])

    def tile_arrival(j):
        part, peer = team(4 - j)
        view = tiles_t.at[pl.ds(part * 16, 16)]
        return remote(view, view, st.at[j], rt.at[j], g, peer)

    for j in range(1, 4):
        cols_copy(j).start()

    @pl.loop(1, 16)
    def _(o):
        plane_copy(o).start()

    for j in range(1, 4):
        tile_copy(j).start()

    own = pltpu.make_async_copy(feat.at[:, :, lanes(f)], slot(1, r), loc.at[8])
    own.start()
    own.wait()
    for copy in ring_copies(0):
        copy.start()

    loads[7].wait()
    for j in range(1, 4):
        cols_arrival(j).wait_recv()
    to_smem = pltpu.make_async_copy(cols_t, cols_s, loc.at[9])
    to_smem.start()

    for i in range(4):
        loads[i].wait()
    feat2 = feat_v[...].reshape(256, 512)
    cot2 = cot_v[...]
    self_part[...] = dot(feat2, w_self[...])
    cot_part[...] = dot_bt(cot2, w_out[...])

    @pl.loop(1, 16)
    def _(o):
        plane_arrival(o).wait_recv()
        for copy in ring_copies(o):
            copy.start()

    to_smem.wait()
    lane = lax.broadcasted_iota(jnp.int32, (8, 128), 1)
    start = jnp.zeros((8, 128), jnp.int32)
    slots = []
    for e in range(64):
        index = window_index(cols_s[e // 16, (e // 8) % 2, e % 8], g)
        slots.append(index)
        start = start + (index < lane).astype(jnp.int32)
        keys[e : e + 1, :] = jnp.full((1, 128), index * 64 + e, jnp.int32)
    all_keys = keys[...]
    rank = jnp.zeros((64, 128), jnp.int32)
    for e in range(64):
        rank = rank + (all_keys > slots[e] * 64 + e).astype(jnp.int32)
    lane64 = lax.broadcasted_iota(jnp.int32, (64, 128), 1)
    entry = lax.broadcasted_iota(jnp.int32, (64, 128), 0)
    order = jnp.sum(jnp.where(rank == lane64, entry, 0), axis=0, keepdims=True)
    table[0:8, :] = jnp.broadcast_to(order, (8, 128))
    table[8:16, :] = start
    to_smem = pltpu.make_async_copy(table, table_s, loc.at[10])
    to_smem.start()
    to_smem.wait()

    loads[6].wait()
    for j in range(1, 4):
        tile_arrival(j).wait_recv()

    @pl.loop(0, 16)
    def _(o):
        for copy in ring_arrivals(o):
            copy.wait_recv()

    def agg_copy(j):
        part, peer = team(j)
        return remote(
            aggq.at[pl.ds(part * 2, 2)], aggr.at[:, :, lanes(f)], sa.at[j], ra.at[j], g, peer
        )

    def agg_arrival(j):
        part, peer = team(4 - j)
        view = aggr.at[:, :, lanes(part)]
        return remote(view, view, sa.at[j], ra.at[j], g, peer)

    def block_sum(part, half_of):
        picked = [win[window_index(cols_s[part, half_of, k], g)] for k in range(8)]
        left = jnp.concatenate([tiles_t[part * 16 + half_of * 8 + k] for k in range(8)], axis=1)
        return dot(left, jnp.concatenate(picked, axis=0)).astype(BF)

    for j in (1, 2, 3, 0):
        part = team(j)[0]
        for half_of in range(2):
            summed = block_sum(part, half_of)
            if j:
                aggq[part * 2 + half_of] = summed
            else:
                aggr[half_of, :, lanes(f)] = summed
        if j:
            agg_copy(j).start()
    loads[4].wait()
    loads[5].wait()
    for j in range(1, 4):
        agg_arrival(j).wait_recv()

    agg = aggr[...].reshape(256, 512)
    pre_first = dot(agg, w_agg[...]) + self_part[...]
    first = (pre_first * jax.nn.sigmoid(pre_first)).astype(BF)
    pre_second = dot(first, w_mid[...])
    second = (pre_second * jax.nn.sigmoid(pre_second)).astype(BF)
    delta_second = (cot_part[...] * silu_slope(pre_second)).astype(BF)
    delta_first = (dot_bt(delta_second, w_mid[...]) * silu_slope(pre_first)).astype(BF)
    dagg[...] = dot_bt(delta_first, w_agg[...]).astype(BF).reshape(2, 128, 512)

    def delta_copy(j):
        part, peer = team(j)
        return remote(
            dagg.at[:, :, lanes(part)], delt.at[pl.ds(f * 2, 2)], sd.at[j], rd.at[j], g, peer
        )

    def delta_arrival(j):
        part, peer = team(4 - j)
        view = delt.at[pl.ds(part * 2, 2)]
        return remote(view, view, sd.at[j], rd.at[j], g, peer)

    for j in range(1, 4):
        delta_copy(j).start()
    delt[pl.ds(f * 2, 2)] = dagg[:, :, lanes(f)]
    grads[0] = dot_at(second, cot2).astype(BF)
    grads[1] = dot_at(first, delta_second).astype(BF)
    grads[2] = dot_at(agg, delta_first).astype(BF)
    grads[3] = dot_at(feat2, delta_first).astype(BF)
    core_copy = remote(grads.at[:, :, lanes(1 - core, 256)], half_in, s_core, r_core, sibling, r)
    core_copy.start()
    for j in range(1, 4):
        delta_arrival(j).wait_recv()

    csum[0] = jnp.zeros((128, 128), F32)

    def add_tiles(i, running):
        for step in range(4):
            e = table_s[0, i * 4 + step]
            running = running + dot_at(tiles_t[e], delt[lax.div(e, 8)])
            csum[i * 4 + step + 1] = running
        return running

    lax.fori_loop(0, 16, add_tiles, jnp.zeros((128, 128), F32))

    def message(w):
        return csum[table_s[8, w + 1]] - csum[table_s[8, w]]

    def message_copies(o):
        s = wrap16(r + o)
        rows = pl.ds(s * 2, 2)
        return (
            remote(to_prior.at[rows], from_next.at[rows], sm.at[0, o], rm.at[0, o], down, r),
            remote(to_next.at[rows], from_prior.at[rows], sm.at[1, o], rm.at[1, o], up, r),
        )

    def message_arrivals(o):
        s = wrap16(r + o)
        a = from_next.at[pl.ds(s * 2, 2)]
        b = from_prior.at[pl.ds(s * 2, 2)]
        return (
            remote(a, a, sm.at[0, o], rm.at[0, o], up, r),
            remote(b, b, sm.at[1, o], rm.at[1, o], down, r),
        )

    @pl.loop(0, 16)
    def _(i):
        o = lax.rem(i + 1, 16)
        s = wrap16(r + o)
        for part in range(2):
            to_prior[s * 2 + part] = message(s * 2 + part).astype(BF)
            to_next[s * 2 + part] = message(64 + s * 2 + part).astype(BF)
        for copy in message_copies(o):
            copy.start()

    core_copy.wait_recv()
    for m in range(4):
        half[m] = (grads[m, :, lanes(core, 256)].astype(F32) + half_in[m].astype(F32)).astype(BF)

    def x_row(j):
        return y_hi * 8 + ((x + j) % 4) * 2 + core

    def x_copy(j):
        return remote(half.at[(x + j) % 4], ring_in.at[j - 1], s_ring.at[j], r_ring.at[j], x_row(j), r)

    for j in range(1, 4):
        x_copy(j).start()

    upd[...] = (feat2.astype(F32) + dot(second, w_out[...])).astype(BF)
    base[...] = (cot2.astype(F32) + dot_bt(delta_first, w_self[...])).reshape(2, 128, 512)

    def return_copy(o):
        s = wrap16(r + o)
        return remote(sums.at[pl.ds(s * 2, 2)], parts.at[pl.ds(r * 2, 2)], sp.at[o], rp.at[o], g, s)

    def return_arrival(o):
        s = wrap16(r - o)
        view = parts.at[pl.ds(s * 2, 2)]
        return remote(view, view, sp.at[o], rp.at[o], g, s)

    def total(s, part):
        i = s * 2 + part
        return (message(32 + i) + from_next[i].astype(F32) + from_prior[i].astype(F32)).astype(BF)

    @pl.loop(1, 16)
    def _(o):
        for copy in message_arrivals(o):
            copy.wait_recv()
        s = wrap16(r + o)
        for part in range(2):
            sums[s * 2 + part] = total(s, part)
        return_copy(o).start()

    for copy in message_arrivals(0):
        copy.wait_recv()
    for part in range(2):
        parts[r * 2 + part] = total(r, part)

    for j in range(1, 4):
        x_copy(j).wait_recv()
    ring[...] = (
        half[x].astype(F32) + ring_in[0].astype(F32) + ring_in[1].astype(F32) + ring_in[2].astype(F32)
    ).astype(BF)
    pair_copy = remote(ring.at[:, lanes(1 - y_hi)], pair_in, s_pair, r_pair, across, r)
    pair_copy.start()
    pair_copy.wait_recv()
    pair[...] = (ring[:, lanes(y_hi)].astype(F32) + pair_in[...].astype(F32)).astype(BF)

    def rep_copy(o):
        s = wrap16(r + o)
        rows = pl.ds(pl.multiple_of(s * 32, 32), 32)
        return remote(pair.at[rows], rep_in.at[o], s_rep.at[o], r_rep.at[o], g, s)

    @pl.loop(1, 16)
    def _(o):
        rep_copy(o).start()

    rep_in[0] = pair[pl.ds(pl.multiple_of(r * 32, 32), 32)]

    @pl.loop(1, 16)
    def _(o):
        return_arrival(o).wait_recv()

    for q in range(4):
        cut = slice(q * 128, q * 128 + 128)
        value = base[:, :, cut]
        for t in range(4):
            s = (q // 2) * 8 + 2 * t + q % 2
            value = value + parts[2 * s : 2 * s + 2].astype(F32)
        gf[:, :, cut] = value.astype(BF)

    @pl.loop(1, 16)
    def _(o):
        rep_copy(o).wait_recv()

    acc = rep_in[0].astype(F32)
    for o in range(1, 16):
        acc = acc + rep_in[o].astype(F32)
    piece[...] = acc * scale

    def place(row):
        return gout.at[(row // 2) % 4, :, lanes((row % 2) * 2 + row // 8)]

    def row_copy(o):
        return remote(piece, place(g), s_row.at[o], r_row.at[o], wrap16(g + o), r)

    def row_arrival(o):
        src = wrap16(g - o)
        return remote(piece, place(src), s_row.at[o], r_row.at[o], src, r)

    @pl.loop(1, 16)
    def _(o):
        row_copy(o).start()

    gout[x, :, lanes(core * 2 + y_hi)] = piece[...]

    @pl.loop(1, 16)
    def _(o):
        row_arrival(o).wait_recv()

    @pl.loop(0, 16)
    def _(o):
        for copy in ring_copies(o) + message_copies(o):
            copy.wait_send()

    @pl.loop(1, 16)
    def _(o):
        plane_copy(o).wait_send()
        return_copy(o).wait_send()
        rep_copy(o).wait_send()
        row_copy(o).wait_send()

    core_copy.wait_send()
    pair_copy.wait_send()
    for j in range(1, 4):
        x_copy(j).wait_send()
        cols_copy(j).wait_send()
        tile_copy(j).wait_send()
        agg_copy(j).wait_send()
        delta_copy(j).wait_send()


def shape(dims, kind):
    return jax.ShapeDtypeStruct(dims, kind)


def local(features, tiles, columns, w_aggregate, w_self, w_middle, w_output, cotangent):
    scale = 1.0 / math.sqrt(features.shape[0] * lax.axis_size("row") * lax.axis_size("rep"))
    weight = VMEM((512, 512), BF)
    panel = VMEM((32, 128, 128), BF)
    upd, gf, gout = pl.pallas_call(
        lambda *refs: layer_kernel(scale, *refs),
        out_shape=(shape((256, 512), BF), shape((2, 128, 512), BF), shape((4, 32, 512), F32)),
        in_specs=[pl.BlockSpec(memory_space=pl.ANY)] * 8,
        out_specs=[pl.BlockSpec(memory_space=VMEM)] * 3,
        scratch_shapes=[
            VMEM((2, 128, 512), BF), VMEM((256, 512), BF), weight, weight, weight, weight,
            VMEM((64, 128, 128), BF), VMEM((4, 2, 8), jnp.int32), VMEM((96, 128, 128), BF),
            pltpu.SMEM((4, 2, 8), jnp.int32), VMEM((64, 128), jnp.int32),
            VMEM((16, 128), jnp.int32), pltpu.SMEM((16, 128), jnp.int32),
            VMEM((8, 128, 128), BF), VMEM((2, 128, 512), BF), VMEM((2, 128, 512), BF),
            VMEM((8, 128, 128), BF), VMEM((256, 512), F32), VMEM((256, 512), F32),
            VMEM((2, 128, 512), F32), VMEM((4, 512, 512), BF), VMEM((65, 128, 128), F32),
            panel, panel, panel, panel, panel, panel,
            VMEM((4, 512, 256), BF), VMEM((4, 512, 256), BF), VMEM((3, 512, 256), BF), VMEM((512, 256), BF),
            VMEM((512, 128), BF), VMEM((512, 128), BF), VMEM((16, 32, 128), BF), VMEM((32, 128), F32),
            DMA((11,)),
            DMA((16,)), DMA((16,)),
            DMA((2, 16)), DMA((2, 16)),
            DMA((4,)), DMA((4,)),
            DMA((4,)), DMA((4,)),
            DMA((4,)), DMA((4,)),
            DMA((4,)), DMA((4,)),
            DMA((2, 16)), DMA((2, 16)),
            DMA((16,)), DMA((16,)),
            DMA, DMA,
            DMA((4,)), DMA((4,)),
            DMA, DMA,
            DMA((16,)), DMA((16,)),
            DMA((16,)), DMA((16,)),
        ],
        compiler_params=pltpu.CompilerParams(
            collective_id=0, has_side_effects=True, vmem_limit_bytes=60 * 1024 * 1024
        ),
        name="message_passing_layer",
    )(
        features.reshape(2, 128, 512), tiles.reshape(16, 128, 128), columns,
        w_aggregate, w_self, w_middle, w_output, cotangent,
    )
    return upd, gf.reshape(256, 512), gout[0], gout[1], gout[2], gout[3]


def solution(mesh):
    placed = (
        P(("row", "rep"), None),
        P(("row", "rep"), None, None, None),
        P(("row", "rep"), None),
        P(),
        P(),
        P(),
        P(),
        P(("row", "rep"), None),
    )
    return jax.shard_map(
        local,
        mesh=mesh,
        in_specs=placed,
        out_specs=(
            P(("row", "rep"), None),
            P(("row", "rep"), None),
            P("rep", None),
            P("rep", None),
            P("rep", None),
            P("rep", None),
        ),
        check_vma=False,
    )
```

time: 139 us -> 124 us (0.89)
  Pallas kernels: 133 us -> 120 us
    pallas_call x3 -> x1, Pallas kernels: 133 us -> 120 us  [local(): pl.pallas_call(lambda *refs: layer_kernel(scale, *refs), out_shape=(shape...]
    unnamed x8 -> x6, local copies, waits for them, and re-layouts: 3.98 us -> 1.75 us
where the time goes in v2:
time: 124 us
  Pallas kernels  120 us (97%)
  local copies, waits for them, and re-layouts  3.43 us (3%)
    pallas_call x1, Pallas kernels, local(): pl.pallas_call(lambda *refs: layer_kernel(scale, *refs), out_shape=(shape...  120 us

profile of v2, /device:TPU:1, one launch (start us, length us, event | category | flops | bytes accessed | tf_op | source)
XLA Modules:
  0.0 124.1 jit_solution(7491666316985418969)
XLA Ops:
  0.6 120.0 %message_passing_layer.1 = (bf16[256,512]{1,0:T(8,128)(2,1)}, bf16[2,128,512]{2,1,0:T(8,128)(2,1)}, f32[4,32,512]{2,1,0:T(8,128)}) custom-call(bf16[2,128,512]{2,1,0:T(8,128)(2,1)} %bitcast.12, bf16[16,128,128]{2,1,0:T(8,128)(2,1)} %bitcast.11, s32[2,8]{1,0:T(2,128)} %refs_2_.1, bf16[512,512]{1,0:T(8,128)(2,1)} %refs_3_.1, bf16[512,512]{1,0:T(8,128)(2,1)} %refs_4_.1, ...), custom_call_target="tpu_custom_call" | custom-call | tf_op jit(solution)/shard_map/message_passing_layer/pallas_call | solution.py:457
  120.7 0.0 copy-start.1
  120.7 1.7 %slice_bitcast_fusion = (f32[32,512]{1,0:T(8,128)}, f32[32,512]{1,0:T(8,128)}, f32[32,512]{1,0:T(8,128)}, f32[32,512]{1,0:T(8,128)}) fusion(f32[4,32,512]{2,1,0:T(8,128)} %get-tuple-element.11), kind=kLoop, calls=%fused_computation | loop fusion | bytes 524288 | tf_op jit(solution)/shard_map/squeeze | solution.py:496
  122.4 0.0 copy-done.1
  122.4 0.0 copy-start
  122.4 0.7 copy.16
  123.1 0.3 copy-done
  123.4 0.7 copy.17
Async XLA Ops:
  120.7 1.7 %copy-start.1 = (bf16[256,512]{1,0:T(8,128)(2,1)S(1)}, bf16[256,512]{1,0:T(8,128)(2,1)}, u32[]{:S(2)}) copy-start(bf16[256,512]{1,0:T(8,128)(2,1)} %get-tuple-element.22) | copy-start | bytes 786436
  122.4 1.0 copy-start

commit v3 on v2

--- a/solution.py
+++ b/solution.py
@@ -12,6 +12,7 @@
 F32 = jnp.float32
 VMEM = pltpu.VMEM
 DMA = pltpu.SemaphoreType.DMA
+HANDED_ALONG_Z = 2
 
 
 def wrap16(value):
@@ -76,7 +77,7 @@
     tiles_t, cols_t, win, cols_s, keys, table, table_s, aggq, aggr, dagg, delt, self_part, cot_part,
     base, grads, csum, to_next, to_prior, from_prior, from_next, sums, parts,
     half_in, half, ring_in, ring, pair_in, pair, rep_in, piece,
-    loc, s1, r1, sx, rx, st, rt, sc, rc, sa, ra, sd, rd,
+    from_mate, loc, s_mate, r_mate, s1, r1, sx, rx, st, rt, sc, rc, sa, ra, sd, rd,
     sm, rm, sp, rp, s_core, r_core, s_ring, r_ring, s_pair, r_pair, s_rep, r_rep, s_row, r_row,
 ):
     g = lax.axis_index("row")
@@ -88,6 +89,9 @@
     up, down = wrap16(g + 1), wrap16(g - 1)
     sibling = g + 1 - 2 * core
     across = (g + 8) % 16
+    y, z = r // 8, r % 8
+    y_mate = (1 - y) * 8 + z
+    z_mate = y * 8 + (z + jnp.where((z + core) % 2 == 0, 1, 7)) % 8
 
     loads = [
         pltpu.make_async_copy(src, dst, loc.at[i])
@@ -101,34 +105,55 @@
     ]
     for load in loads:
         load.start()
-    greet([(g, wrap16(r + o)) for o in range(1, 16)] + [(wrap16(g + o), r) for o in range(1, 16)])
+    greet([(g, wrap16(r + o)) for o in range(1, 16)] + [(wrap16(g + o), r) for o in range(1, 16)] + [(across, y_mate)])
 
     def slot(panel, rep):
         return win.at[pl.ds(panel * 32 + rep * 2, 2)]
 
-    def plane_copy(o):
-        peer = wrap16(r + o)
-        return remote(
-            feat.at[:, :, lanes(quarter(peer))], slot(1, r), s1.at[o], r1.at[o], g, peer
-        )
-
-    def plane_arrival(o):
-        src = wrap16(r - o)
-        return remote(slot(1, src), slot(1, src), s1.at[o], r1.at[o], g, src)
-
-    def ring_copies(o):
-        src = wrap16(r - o)
+    def source(row, d):
+        return jnp.where(row == 0, y, 1 - y) * 8 + (z - d + 8) % 8
+
+    def mate_copy():
+        return remote(feat.at[:, :, lanes(1 - y, 256)], from_mate, s_mate, r_mate, g, y_mate)
+
+    def chunk_copy(row, d, held=0):
+        peer = y * 8 + (z - held + d) % 8
+        if held:
+            src = slot(1, source(row, held))
+        else:
+            src = (feat, from_mate)[row].at[:, :, lanes(quarter(peer) if row == 0 else peer % 2)]
+        dst = slot(1, source(row, held))
+        return remote(src, dst, s1.at[row, d], r1.at[row, d], g, peer)
+
+    def chunk_arrival(row, d):
+        view = slot(1, source(row, d))
+        return remote(view, view, s1.at[row, d], r1.at[row, d], g, y * 8 + (z - d + 8) % 8)
+
+    def ring_copies(row, d):
+        src = source(row, d)
         return (
-            remote(slot(1, src), slot(0, src), sx.at[0, o], rx.at[0, o], up, r),
-            remote(slot(1, src), slot(2, src), sx.at[1, o], rx.at[1, o], down, r),
-        )
-
-    def ring_arrivals(o):
-        src = wrap16(r - o)
+            remote(slot(1, src), slot(0, src), sx.at[row, d, 0], rx.at[row, d, 0], up, r),
+            remote(slot(1, src), slot(2, src), sx.at[row, d, 1], rx.at[row, d, 1], down, r),
+        )
+
+    def ring_arrivals(row, d):
+        src = source(row, d)
         return (
-            remote(slot(0, src), slot(0, src), sx.at[0, o], rx.at[0, o], down, r),
-            remote(slot(2, src), slot(2, src), sx.at[1, o], rx.at[1, o], up, r),
-        )
+            remote(slot(0, src), slot(0, src), sx.at[row, d, 0], rx.at[row, d, 0], down, r),
+            remote(slot(2, src), slot(2, src), sx.at[row, d, 1], rx.at[row, d, 1], up, r),
+        )
+
+    def send_ring(row, d):
+        for copy in ring_copies(row, d):
+            copy.start()
+
+    def pass_on(row, d):
+        chunk_arrival(row, d).wait_recv()
+        if d in (1, 7):
+            chunk_copy(row, 3 if d == 1 else 5, held=d).start()
+        if d == (2 if row == 0 else 6):
+            chunk_copy(row, 4, held=d).start()
+        send_ring(row, d)
 
     def team(j):
         part = (f + j) % 4
@@ -141,29 +166,54 @@
         part, peer = team(4 - j)
         return remote(cols_t.at[part], cols_t.at[part], sc.at[j], rc.at[j], g, peer)
 
-    def tile_copy(j):
-        return remote(tiles, tiles_t.at[pl.ds(f * 16, 16)], st.at[j], rt.at[j], g, team(j)[1])
-
-    def tile_arrival(j):
-        part, peer = team(4 - j)
-        view = tiles_t.at[pl.ds(part * 16, 16)]
-        return remote(view, view, st.at[j], rt.at[j], g, peer)
+    def piece_of(rep, i):
+        return tiles_t.at[pl.ds(quarter(rep) * 16 + i * 4, 4)]
+
+    def tile_copy(way, i):
+        peer = (y_mate, z_mate)[way]
+        return remote(tiles.at[pl.ds(i * 4, 4)], piece_of(r, i), st.at[way, i], rt.at[way, i], g, peer)
+
+    def tile_arrival(way, i):
+        peer = (y_mate, z_mate)[way]
+        return remote(piece_of(peer, i), piece_of(peer, i), st.at[way, i], rt.at[way, i], g, peer)
+
+    def hand_copy(i):
+        src, peer = (y_mate, z_mate) if i < HANDED_ALONG_Z else (z_mate, y_mate)
+        return remote(piece_of(src, i), piece_of(src, i), st.at[2, i], rt.at[2, i], g, peer)
+
+    def hand_arrival(i):
+        far = mate(r, core, 3 - f)
+        peer = z_mate if i < HANDED_ALONG_Z else y_mate
+        return remote(piece_of(far, i), piece_of(far, i), st.at[2, i], rt.at[2, i], g, peer)
 
     for j in range(1, 4):
         cols_copy(j).start()
 
-    @pl.loop(1, 16)
-    def _(o):
-        plane_copy(o).start()
-
-    for j in range(1, 4):
-        tile_copy(j).start()
-
+    mate_copy().start()
+    for d in (1, 7, 2, 6):
+        chunk_copy(0, d).start()
+    for i in range(4):
+        tile_copy(0, i).start()
+    for i in range(HANDED_ALONG_Z, 4):
+        tile_copy(1, i).start()
     own = pltpu.make_async_copy(feat.at[:, :, lanes(f)], slot(1, r), loc.at[8])
     own.start()
     own.wait()
-    for copy in ring_copies(0):
-        copy.start()
+    send_ring(0, 0)
+    mate_copy().wait_recv()
+    for d in (1, 7, 2, 6):
+        chunk_copy(1, d).start()
+    for i in range(HANDED_ALONG_Z):
+        tile_copy(1, i).start()
+    own = pltpu.make_async_copy(from_mate.at[:, :, lanes(z % 2)], slot(1, y_mate), loc.at[11])
+    own.start()
+    own.wait()
+    send_ring(1, 0)
+    for d in (1, 7, 2, 6):
+        pass_on(0, d)
+    for i in range(HANDED_ALONG_Z):
+        tile_arrival(0, i).wait_recv()
+        hand_copy(i).start()
 
     loads[7].wait()
     for j in range(1, 4):
@@ -178,11 +228,11 @@
     self_part[...] = dot(feat2, w_self[...])
     cot_part[...] = dot_bt(cot2, w_out[...])
 
-    @pl.loop(1, 16)
-    def _(o):
-        plane_arrival(o).wait_recv()
-        for copy in ring_copies(o):
-            copy.start()
+    for d in (1, 7, 2, 6):
+        pass_on(1, d)
+    for i in range(HANDED_ALONG_Z, 4):
+        tile_arrival(1, i).wait_recv()
+        hand_copy(i).start()
 
     to_smem.wait()
     lane = lax.broadcasted_iota(jnp.int32, (8, 128), 1)
@@ -206,14 +256,20 @@
     to_smem.start()
     to_smem.wait()
 
+    for d in (3, 5, 4):
+        for row in range(2):
+            pass_on(row, d)
     loads[6].wait()
-    for j in range(1, 4):
-        tile_arrival(j).wait_recv()
-
-    @pl.loop(0, 16)
-    def _(o):
-        for copy in ring_arrivals(o):
-            copy.wait_recv()
+    for i in range(HANDED_ALONG_Z, 4):
+        tile_arrival(0, i).wait_recv()
+    for i in range(HANDED_ALONG_Z):
+        tile_arrival(1, i).wait_recv()
+    for i in range(4):
+        hand_arrival(i).wait_recv()
+    for d in range(8):
+        for row in range(2):
+            for copy in ring_arrivals(row, d):
+                copy.wait_recv()
 
     def agg_copy(j):
         part, peer = team(j)
@@ -323,14 +379,13 @@
     for m in range(4):
         half[m] = (grads[m, :, lanes(core, 256)].astype(F32) + half_in[m].astype(F32)).astype(BF)
 
-    def x_row(j):
-        return y_hi * 8 + ((x + j) % 4) * 2 + core
-
-    def x_copy(j):
-        return remote(half.at[(x + j) % 4], ring_in.at[j - 1], s_ring.at[j], r_ring.at[j], x_row(j), r)
-
-    for j in range(1, 4):
-        x_copy(j).start()
+    def y_copy(j):
+        row, rep = across if j & 2 else g, y_mate if j & 1 else r
+        rows = pl.ds(pl.multiple_of((rep // 8) * 256, 256), 256)
+        return remote(half.at[:, rows, lanes(row // 8)], pair_in.at[j - 1], s_pair.at[j], r_pair.at[j], row, rep)
+
+    for j in range(1, 4):
+        y_copy(j).start()
 
     upd[...] = (feat2.astype(F32) + dot(second, w_out[...])).astype(BF)
     base[...] = (cot2.astype(F32) + dot_bt(delta_first, w_self[...])).reshape(2, 128, 512)
@@ -363,25 +418,56 @@
         parts[r * 2 + part] = total(r, part)
 
     for j in range(1, 4):
+        y_copy(j).wait_recv()
+    own_rows = pl.ds(pl.multiple_of(y * 256, 256), 256)
+    for m in range(4):
+        value = half[m, own_rows, lanes(y_hi)].astype(F32)
+        for j in range(3):
+            value = value + pair_in[j, m].astype(F32)
+        pair[m] = value.astype(BF)
+
+    def x_row(j):
+        return y_hi * 8 + ((x + j) % 4) * 2 + core
+
+    def x_copy(j):
+        return remote(pair.at[(x + j) % 4], ring_in.at[j - 1], s_ring.at[j], r_ring.at[j], x_row(j), r)
+
+    for j in range(1, 4):
+        x_copy(j).start()
+    for j in range(1, 4):
         x_copy(j).wait_recv()
     ring[...] = (
-        half[x].astype(F32) + ring_in[0].astype(F32) + ring_in[1].astype(F32) + ring_in[2].astype(F32)
+        pair[x].astype(F32) + ring_in[0].astype(F32) + ring_in[1].astype(F32) + ring_in[2].astype(F32)
     ).astype(BF)
-    pair_copy = remote(ring.at[:, lanes(1 - y_hi)], pair_in, s_pair, r_pair, across, r)
-    pair_copy.start()
-    pair_copy.wait_recv()
-    pair[...] = (ring[:, lanes(y_hi)].astype(F32) + pair_in[...].astype(F32)).astype(BF)
-
-    def rep_copy(o):
-        s = wrap16(r + o)
-        rows = pl.ds(pl.multiple_of(s * 32, 32), 32)
-        return remote(pair.at[rows], rep_in.at[o], s_rep.at[o], r_rep.at[o], g, s)
+
+    def rep_copy(d):
+        to = (z + d) % 8
+        rows = pl.ds(pl.multiple_of(to * 32, 32), 32)
+        return remote(ring.at[rows], rep_in.at[d], s_rep.at[d], r_rep.at[d], g, y * 8 + to)
+
+    for d in range(1, 8):
+        rep_copy(d).start()
+    acc = ring[pl.ds(pl.multiple_of(z * 32, 32), 32)].astype(F32)
+    for d in range(1, 8):
+        rep_copy(d).wait_recv()
+        acc = acc + rep_in[d].astype(F32)
+    piece[...] = acc * scale
+
+    def place(row):
+        return gout.at[(row // 2) % 4, :, lanes((row % 2) * 2 + row // 8)]
+
+    def row_copy(o):
+        return remote(piece, place(g), s_row.at[o], r_row.at[o], wrap16(g + o), r)
+
+    def row_arrival(o):
+        src = wrap16(g - o)
+        return remote(piece, place(src), s_row.at[o], r_row.at[o], src, r)
 
     @pl.loop(1, 16)
     def _(o):
-        rep_copy(o).start()
-
-    rep_in[0] = pair[pl.ds(pl.multiple_of(r * 32, 32), 32)]
+        row_copy(o).start()
+
+    gout[x, :, lanes(core * 2 + y_hi)] = piece[...]
 
     @pl.loop(1, 16)
     def _(o):
@@ -397,53 +483,41 @@
 
     @pl.loop(1, 16)
     def _(o):
-        rep_copy(o).wait_recv()
-
-    acc = rep_in[0].astype(F32)
-    for o in range(1, 16):
-        acc = acc + rep_in[o].astype(F32)
-    piece[...] = acc * scale
-
-    def place(row):
-        return gout.at[(row // 2) % 4, :, lanes((row % 2) * 2 + row // 8)]
-
-    def row_copy(o):
-        return remote(piece, place(g), s_row.at[o], r_row.at[o], wrap16(g + o), r)
-
-    def row_arrival(o):
-        src = wrap16(g - o)
-        return remote(piece, place(src), s_row.at[o], r_row.at[o], src, r)
+        row_arrival(o).wait_recv()
+
+    @pl.loop(0, 16)
+    def _(o):
+        for copy in message_copies(o):
+            copy.wait_send()
 
     @pl.loop(1, 16)
     def _(o):
-        row_copy(o).start()
-
-    gout[x, :, lanes(core * 2 + y_hi)] = piece[...]
-
-    @pl.loop(1, 16)
-    def _(o):
-        row_arrival(o).wait_recv()
-
-    @pl.loop(0, 16)
-    def _(o):
-        for copy in ring_copies(o) + message_copies(o):
-            copy.wait_send()
-
-    @pl.loop(1, 16)
-    def _(o):
-        plane_copy(o).wait_send()
         return_copy(o).wait_send()
-        rep_copy(o).wait_send()
         row_copy(o).wait_send()
 
+    mate_copy().wait_send()
+    for row in range(2):
+        for d in (1, 7, 2, 6):
+            chunk_copy(row, d).wait_send()
+        chunk_copy(row, 3, held=1).wait_send()
+        chunk_copy(row, 5, held=7).wait_send()
+        chunk_copy(row, 4, held=2 if row == 0 else 6).wait_send()
+        for d in range(8):
+            for copy in ring_copies(row, d):
+                copy.wait_send()
+    for i in range(4):
+        tile_copy(0, i).wait_send()
+        tile_copy(1, i).wait_send()
+        hand_copy(i).wait_send()
     core_copy.wait_send()
-    pair_copy.wait_send()
-    for j in range(1, 4):
+    for j in range(1, 4):
+        y_copy(j).wait_send()
         x_copy(j).wait_send()
         cols_copy(j).wait_send()
-        tile_copy(j).wait_send()
         agg_copy(j).wait_send()
         delta_copy(j).wait_send()
+    for d in range(1, 8):
+        rep_copy(d).wait_send()
 
 
 def shape(dims, kind):
@@ -457,7 +531,7 @@
     upd, gf, gout = pl.pallas_call(
         lambda *refs: layer_kernel(scale, *refs),
         out_shape=(shape((256, 512), BF), shape((2, 128, 512), BF), shape((4, 32, 512), F32)),
-        in_specs=[pl.BlockSpec(memory_space=pl.ANY)] * 8,
+        in_specs=[pl.BlockSpec(memory_space=pltpu.HBM)] * 8,
         out_specs=[pl.BlockSpec(memory_space=VMEM)] * 3,
         scratch_shapes=[
             VMEM((2, 128, 512), BF), VMEM((256, 512), BF), weight, weight, weight, weight,
@@ -468,12 +542,13 @@
             VMEM((8, 128, 128), BF), VMEM((256, 512), F32), VMEM((256, 512), F32),
             VMEM((2, 128, 512), F32), VMEM((4, 512, 512), BF), VMEM((65, 128, 128), F32),
             panel, panel, panel, panel, panel, panel,
-            VMEM((4, 512, 256), BF), VMEM((4, 512, 256), BF), VMEM((3, 512, 256), BF), VMEM((512, 256), BF),
-            VMEM((512, 128), BF), VMEM((512, 128), BF), VMEM((16, 32, 128), BF), VMEM((32, 128), F32),
-            DMA((11,)),
-            DMA((16,)), DMA((16,)),
-            DMA((2, 16)), DMA((2, 16)),
-            DMA((4,)), DMA((4,)),
+            VMEM((4, 512, 256), BF), VMEM((4, 512, 256), BF), VMEM((3, 256, 128), BF), VMEM((256, 128), BF),
+            VMEM((3, 4, 256, 128), BF), VMEM((4, 256, 128), BF), VMEM((8, 32, 128), BF), VMEM((32, 128), F32),
+            VMEM((2, 128, 256), BF),
+            DMA((12,)), DMA, DMA,
+            DMA((2, 8)), DMA((2, 8)),
+            DMA((2, 8, 2)), DMA((2, 8, 2)),
+            DMA((3, 4)), DMA((3, 4)),
             DMA((4,)), DMA((4,)),
             DMA((4,)), DMA((4,)),
             DMA((4,)), DMA((4,)),
@@ -481,12 +556,12 @@
             DMA((16,)), DMA((16,)),
             DMA, DMA,
             DMA((4,)), DMA((4,)),
-            DMA, DMA,
-            DMA((16,)), DMA((16,)),
+            DMA((4,)), DMA((4,)),
+            DMA((8,)), DMA((8,)),
             DMA((16,)), DMA((16,)),
         ],
         compiler_params=pltpu.CompilerParams(
-            collective_id=0, has_side_effects=True, vmem_limit_bytes=60 * 1024 * 1024
+            collective_id=0, has_side_effects=True, vmem_limit_bytes=52 * 1024 * 1024
         ),
         name="message_passing_layer",
     )(

time: 124 us -> 119 us (0.960)
  Pallas kernels: 120 us -> 112 us
  local copies, waits for them, and re-layouts: 3.43 us -> 5.72 us
    pallas_call x1, Pallas kernels: 120 us -> 112 us  [local(): pl.pallas_call(lambda *refs: layer_kernel(scale, *refs), out_shape=(shape...]
    unnamed x6 -> x10, local copies, waits for them, and re-layouts: 1.75 us -> 5.02 us
where the time goes in v3:
time: 119 us
  Pallas kernels  112 us (94%)
  local copies, waits for them, and re-layouts  5.72 us (5%)
    pallas_call x1, Pallas kernels, local(): pl.pallas_call(lambda *refs: layer_kernel(scale, *refs), out_shape=(shape...  112 us
    unnamed x10, local copies, waits for them, and re-layouts  5.02 us

profile of v3, /device:TPU:1, one launch (start us, length us, event | category | flops | bytes accessed | tf_op | source)
XLA Modules:
  0.0 118.5 jit_solution(1611010264873284356)
XLA Ops:
  0.6 0.0 copy-start.3
  0.6 0.7 copy-done.3
  1.3 0.0 copy-start
  1.3 1.0 copy-done
  2.4 0.0 copy-start.1
  2.4 0.9 copy-done.1
  3.3 0.0 copy-start.2
  3.3 0.9 copy-done.2
  4.3 112.2 %message_passing_layer.1 = (bf16[256,512]{1,0:T(8,128)(2,1)S(1)}, bf16[2,128,512]{2,1,0:T(8,128)(2,1)S(1)}, f32[4,32,512]{2,1,0:T(8,128)S(1)}) custom-call(bf16[2,128,512]{2,1,0:T(8,128)(2,1)S(1)} %bitcast.12, bf16[16,128,128]{2,1,0:T(8,128)(2,1)S(1)} %bitcast.11, s32[2,8]{1,0:T(2,128)S(1)} %copy-done.3, bf16[512,512]{1,0:T(8,128)(2,1)} %refs_3_.1, ...), custom_call_target="tpu_custom_call" | custom-call | tf_op jit(solution)/shard_map/message_passing_layer/pallas_call | solution.py:531
  116.4 0.7 slice_bitcast_fusion
  117.1 0.7 copy.16
  117.8 0.7 copy.17
Async XLA Ops:
  0.6 0.7 copy-start.3
  1.3 1.0 copy-start
  2.4 0.9 copy-start.1
  3.3 0.9 copy-start.2

commit v4 on v3

--- a/solution.py
+++ b/solution.py
@@ -13,6 +13,7 @@
 VMEM = pltpu.VMEM
 DMA = pltpu.SemaphoreType.DMA
 HANDED_ALONG_Z = 2
+Y_SUM_AT, X_SUM_AT = 8, 12
 
 
 def wrap16(value):
@@ -325,12 +326,28 @@
     for j in range(1, 4):
         delta_copy(j).start()
     delt[pl.ds(f * 2, 2)] = dagg[:, :, lanes(f)]
-    grads[0] = dot_at(second, cot2).astype(BF)
-    grads[1] = dot_at(first, delta_second).astype(BF)
-    grads[2] = dot_at(agg, delta_first).astype(BF)
-    grads[3] = dot_at(feat2, delta_first).astype(BF)
-    core_copy = remote(grads.at[:, :, lanes(1 - core, 256)], half_in, s_core, r_core, sibling, r)
-    core_copy.start()
+
+    def core_copy(m):
+        return remote(grads.at[m, :, lanes(1 - core, 256)], half_in.at[m], s_core.at[m], r_core.at[m], sibling, r)
+
+    for m, (a, b) in enumerate(((second, cot2), (first, delta_second), (agg, delta_first), (feat2, delta_first))):
+        grads[m] = dot_at(a, b).astype(BF)
+        core_copy(m).start()
+    upd[...] = (feat2.astype(F32) + dot(second, w_out[...])).astype(BF)
+    base[...] = (cot2.astype(F32) + dot_bt(delta_first, w_self[...])).reshape(2, 128, 512)
+
+    for m in range(4):
+        core_copy(m).wait_recv()
+        half[m] = (grads[m, :, lanes(core, 256)].astype(F32) + half_in[m].astype(F32)).astype(BF)
+
+    def y_copy(j):
+        row, rep = across if j & 2 else g, y_mate if j & 1 else r
+        rows = pl.ds(pl.multiple_of((rep // 8) * 256, 256), 256)
+        return remote(half.at[:, rows, lanes(row // 8)], pair_in.at[j - 1], s_pair.at[j], r_pair.at[j], row, rep)
+
+    for j in range(1, 4):
+        y_copy(j).start()
+
     for j in range(1, 4):
         delta_arrival(j).wait_recv()
 
@@ -375,21 +392,6 @@
         for copy in message_copies(o):
             copy.start()
 
-    core_copy.wait_recv()
-    for m in range(4):
-        half[m] = (grads[m, :, lanes(core, 256)].astype(F32) + half_in[m].astype(F32)).astype(BF)
-
-    def y_copy(j):
-        row, rep = across if j & 2 else g, y_mate if j & 1 else r
-        rows = pl.ds(pl.multiple_of((rep // 8) * 256, 256), 256)
-        return remote(half.at[:, rows, lanes(row // 8)], pair_in.at[j - 1], s_pair.at[j], r_pair.at[j], row, rep)
-
-    for j in range(1, 4):
-        y_copy(j).start()
-
-    upd[...] = (feat2.astype(F32) + dot(second, w_out[...])).astype(BF)
-    base[...] = (cot2.astype(F32) + dot_bt(delta_first, w_self[...])).reshape(2, 128, 512)
-
     def return_copy(o):
         s = wrap16(r + o)
         return remote(sums.at[pl.ds(s * 2, 2)], parts.at[pl.ds(r * 2, 2)], sp.at[o], rp.at[o], g, s)
@@ -403,8 +405,7 @@
         i = s * 2 + part
         return (message(32 + i) + from_next[i].astype(F32) + from_prior[i].astype(F32)).astype(BF)
 
-    @pl.loop(1, 16)
-    def _(o):
+    def send_back(o):
         for copy in message_arrivals(o):
             copy.wait_recv()
         s = wrap16(r + o)
@@ -412,11 +413,7 @@
             sums[s * 2 + part] = total(s, part)
         return_copy(o).start()
 
-    for copy in message_arrivals(0):
-        copy.wait_recv()
-    for part in range(2):
-        parts[r * 2 + part] = total(r, part)
-
+    pl.loop(1, Y_SUM_AT)(send_back)
     for j in range(1, 4):
         y_copy(j).wait_recv()
     own_rows = pl.ds(pl.multiple_of(y * 256, 256), 256)
@@ -434,6 +431,7 @@
 
     for j in range(1, 4):
         x_copy(j).start()
+    pl.loop(Y_SUM_AT, X_SUM_AT)(send_back)
     for j in range(1, 4):
         x_copy(j).wait_recv()
     ring[...] = (
@@ -447,6 +445,12 @@
 
     for d in range(1, 8):
         rep_copy(d).start()
+    pl.loop(X_SUM_AT, 16)(send_back)
+    for copy in message_arrivals(0):
+        copy.wait_recv()
+    for part in range(2):
+        parts[r * 2 + part] = total(r, part)
+
     acc = ring[pl.ds(pl.multiple_of(z * 32, 32), 32)].astype(F32)
     for d in range(1, 8):
         rep_copy(d).wait_recv()
@@ -509,7 +513,8 @@
         tile_copy(0, i).wait_send()
         tile_copy(1, i).wait_send()
         hand_copy(i).wait_send()
-    core_copy.wait_send()
+    for m in range(4):
+        core_copy(m).wait_send()
     for j in range(1, 4):
         y_copy(j).wait_send()
         x_copy(j).wait_send()
@@ -554,7 +559,7 @@
             DMA((4,)), DMA((4,)),
             DMA((2, 16)), DMA((2, 16)),
             DMA((16,)), DMA((16,)),
-            DMA, DMA,
+            DMA((4,)), DMA((4,)),
             DMA((4,)), DMA((4,)),
             DMA((4,)), DMA((4,)),
             DMA((8,)), DMA((8,)),
@@ -565,8 +570,13 @@
         ),
         name="message_passing_layer",
     )(
-        features.reshape(2, 128, 512), tiles.reshape(16, 128, 128), columns,
-        w_aggregate, w_self, w_middle, w_output, cotangent,
+        *(
+            pltpu.with_memory_space_constraint(value, pltpu.HBM)
+            for value in (
+                features.reshape(2, 128, 512), tiles.reshape(16, 128, 128), columns,
+                w_aggregate, w_self, w_middle, w_output, cotangent,
+            )
+        )
     )
     return upd, gf.reshape(256, 512), gout[0], gout[1], gout[2], gout[3]
 

time: 119 us -> 111 us (0.933)
  Pallas kernels: 112 us -> 107 us
  local copies, waits for them, and re-layouts: 5.72 us -> 2.11 us
    pallas_call x1, Pallas kernels: 112 us -> 107 us  [local(): pl.pallas_call(lambda *refs: layer_kernel(scale, *refs), out_shape=(shape...]
    unnamed x10 -> x2, local copies, waits for them, and re-layouts: 5.02 us -> 1.4 us
where the time goes in v4:
time: 111 us; the launch traced here: 110 us
  Pallas kernels  107 us (96%)
  local copies, waits for them, and re-layouts  2.11 us (2%)
    pallas_call x1, Pallas kernels, local(): pl.pallas_call(lambda *refs: layer_kernel(scale, *refs), out_shape=(shape...  107 us

profile of v4, /device:TPU:1, one launch (start us, length us, event | category | flops | bytes accessed | tf_op | source)
XLA Modules:
  0.0 109.8 jit_solution(12595862009173809691)
XLA Ops:
  0.6 107.0 %message_passing_layer.1 = (bf16[256,512]{1,0:T(8,128)(2,1)S(1)}, bf16[2,128,512]{2,1,0:T(8,128)(2,1)S(1)}, f32[4,32,512]{2,1,0:T(8,128)S(1)}) custom-call(bf16[2,128,512]{2,1,0:T(8,128)(2,1)} %bitcast.13, bf16[16,128,128]{2,1,0:T(8,128)(2,1)} %bitcast.12, s32[2,8]{1,0:T(2,128)} %refs_2_.1, bf16[512,512]{1,0:T(8,128)(2,1)} %refs_3_.1, ...), custom_call_target="tpu_custom_call" | custom-call | tf_op jit(solution)/shard_map/message_passing_layer/pallas_call | solution.py:536
  107.7 0.7 slice_bitcast_fusion
  108.4 0.7 copy.16
  109.1 0.7 copy.17

commit v5 on v4

--- a/solution.py
+++ b/solution.py
@@ -77,9 +77,9 @@
     feat_v, cot_v, w_agg, w_self, w_mid, w_out,
     tiles_t, cols_t, win, cols_s, keys, table, table_s, aggq, aggr, dagg, delt, self_part, cot_part,
     base, grads, csum, to_next, to_prior, from_prior, from_next, sums, parts,
-    half_in, half, ring_in, ring, pair_in, pair, rep_in, piece,
+    half_in, half, a_in, b_in, a_sum, b_sum, a2_in, b2_in, last, rep_in, piece,
     from_mate, loc, s_mate, r_mate, s1, r1, sx, rx, st, rt, sc, rc, sa, ra, sd, rd,
-    sm, rm, sp, rp, s_core, r_core, s_ring, r_ring, s_pair, r_pair, s_rep, r_rep, s_row, r_row,
+    sm, rm, sp, rp, s_core, r_core, s_a, r_a, s_b, r_b, s_a2, r_a2, s_b2, r_b2, s_rep, r_rep, s_row, r_row,
 ):
     g = lax.axis_index("row")
     r = lax.axis_index("rep")
@@ -338,15 +338,43 @@
 
     for m in range(4):
         core_copy(m).wait_recv()
-        half[m] = (grads[m, :, lanes(core, 256)].astype(F32) + half_in[m].astype(F32)).astype(BF)
-
-    def y_copy(j):
-        row, rep = across if j & 2 else g, y_mate if j & 1 else r
-        rows = pl.ds(pl.multiple_of((rep // 8) * 256, 256), 256)
-        return remote(half.at[:, rows, lanes(row // 8)], pair_in.at[j - 1], s_pair.at[j], r_pair.at[j], row, rep)
-
-    for j in range(1, 4):
-        y_copy(j).start()
+        value = (grads[m, :, lanes(core, 256)].astype(F32) + half_in[m].astype(F32)).astype(BF)
+        half[m] = value.reshape(16, 2, 16, 256)
+
+    def y_peer(j):
+        return across if j & 2 else g, y_mate if j & 1 else r
+
+    def y_part(row, rep):
+        return pl.ds((rep // 8) * 8, 8), lanes(row // 8)
+
+    def x_peer(j):
+        to = (x + j) % 4
+        return y_hi * 8 + to * 2 + core, to
+
+    def a_copy(j):
+        row, rep = y_peer(j)
+        rows, columns = y_part(row, rep)
+        src = half.at[0:2, rows, :, :, columns]
+        return remote(src, a_in.at[j - 1], s_a.at[j], r_a.at[j], row, rep)
+
+    def b_copy(j):
+        row, to = x_peer(j)
+        src = half.at[2 + to // 2, :, to % 2]
+        return remote(src, b_in.at[j - 1], s_b.at[j], r_b.at[j], row, r)
+
+    def a2_copy(j):
+        row, to = x_peer(j)
+        return remote(a_sum.at[to // 2, :, to % 2], a2_in.at[j - 1], s_a2.at[j], r_a2.at[j], row, r)
+
+    def b2_copy(j):
+        row, rep = y_peer(j)
+        rows, columns = y_part(row, rep)
+        return remote(b_sum.at[rows, :, columns], b2_in.at[j - 1], s_b2.at[j], r_b2.at[j], row, rep)
+
+    own_rows, own_columns = y_part(g, r)
+    for j in range(1, 4):
+        a_copy(j).start()
+        b_copy(j).start()
 
     for j in range(1, 4):
         delta_arrival(j).wait_recv()
@@ -415,33 +443,35 @@
 
     pl.loop(1, Y_SUM_AT)(send_back)
     for j in range(1, 4):
-        y_copy(j).wait_recv()
-    own_rows = pl.ds(pl.multiple_of(y * 256, 256), 256)
-    for m in range(4):
-        value = half[m, own_rows, lanes(y_hi)].astype(F32)
+        a_copy(j).wait_recv()
+        b_copy(j).wait_recv()
+    for m in range(2):
+        value = half[m, own_rows, :, :, own_columns].astype(F32)
         for j in range(3):
-            value = value + pair_in[j, m].astype(F32)
-        pair[m] = value.astype(BF)
-
-    def x_row(j):
-        return y_hi * 8 + ((x + j) % 4) * 2 + core
-
-    def x_copy(j):
-        return remote(pair.at[(x + j) % 4], ring_in.at[j - 1], s_ring.at[j], r_ring.at[j], x_row(j), r)
-
-    for j in range(1, 4):
-        x_copy(j).start()
+            value = value + a_in[j, m].astype(F32)
+        a_sum[m] = value.astype(BF)
+    value = half[2 + x // 2, :, x % 2].astype(F32)
+    for j in range(3):
+        value = value + b_in[j].astype(F32)
+    b_sum[...] = value.astype(BF)
+    for j in range(1, 4):
+        a2_copy(j).start()
+        b2_copy(j).start()
     pl.loop(Y_SUM_AT, X_SUM_AT)(send_back)
     for j in range(1, 4):
-        x_copy(j).wait_recv()
-    ring[...] = (
-        pair[x].astype(F32) + ring_in[0].astype(F32) + ring_in[1].astype(F32) + ring_in[2].astype(F32)
-    ).astype(BF)
+        a2_copy(j).wait_recv()
+        b2_copy(j).wait_recv()
+    a_value = a_sum[x // 2, :, x % 2].astype(F32)
+    b_value = b_sum[own_rows, :, own_columns].astype(F32)
+    for j in range(3):
+        a_value = a_value + a2_in[j].astype(F32)
+        b_value = b_value + b2_in[j].astype(F32)
+    last[:, 0] = a_value.astype(BF)
+    last[:, 1] = b_value.astype(BF)
 
     def rep_copy(d):
         to = (z + d) % 8
-        rows = pl.ds(pl.multiple_of(to * 32, 32), 32)
-        return remote(ring.at[rows], rep_in.at[d], s_rep.at[d], r_rep.at[d], g, y * 8 + to)
+        return remote(last.at[to], rep_in.at[d], s_rep.at[d], r_rep.at[d], g, y * 8 + to)
 
     for d in range(1, 8):
         rep_copy(d).start()
@@ -451,14 +481,16 @@
     for part in range(2):
         parts[r * 2 + part] = total(r, part)
 
-    acc = ring[pl.ds(pl.multiple_of(z * 32, 32), 32)].astype(F32)
+    acc = last[z].astype(F32)
     for d in range(1, 8):
         rep_copy(d).wait_recv()
         acc = acc + rep_in[d].astype(F32)
     piece[...] = acc * scale
 
     def place(row):
-        return gout.at[(row // 2) % 4, :, lanes((row % 2) * 2 + row // 8)]
+        to = (row // 2) % 4
+        rows = pl.ds(pl.multiple_of((to % 2) * 16, 16), 16)
+        return gout.at[:, to // 2, rows, lanes((row % 2) * 2 + row // 8)]
 
     def row_copy(o):
         return remote(piece, place(g), s_row.at[o], r_row.at[o], wrap16(g + o), r)
@@ -471,7 +503,8 @@
     def _(o):
         row_copy(o).start()
 
-    gout[x, :, lanes(core * 2 + y_hi)] = piece[...]
+    rows = pl.ds(pl.multiple_of((x % 2) * 16, 16), 16)
+    gout[:, x // 2, rows, lanes(core * 2 + y_hi)] = piece[...]
 
     @pl.loop(1, 16)
     def _(o):
@@ -516,8 +549,10 @@
     for m in range(4):
         core_copy(m).wait_send()
     for j in range(1, 4):
-        y_copy(j).wait_send()
-        x_copy(j).wait_send()
+        a_copy(j).wait_send()
+        b_copy(j).wait_send()
+        a2_copy(j).wait_send()
+        b2_copy(j).wait_send()
         cols_copy(j).wait_send()
         agg_copy(j).wait_send()
         delta_copy(j).wait_send()
@@ -535,7 +570,7 @@
     panel = VMEM((32, 128, 128), BF)
     upd, gf, gout = pl.pallas_call(
         lambda *refs: layer_kernel(scale, *refs),
-        out_shape=(shape((256, 512), BF), shape((2, 128, 512), BF), shape((4, 32, 512), F32)),
+        out_shape=(shape((256, 512), BF), shape((2, 128, 512), BF), shape((2, 2, 32, 512), F32)),
         in_specs=[pl.BlockSpec(memory_space=pltpu.HBM)] * 8,
         out_specs=[pl.BlockSpec(memory_space=VMEM)] * 3,
         scratch_shapes=[
@@ -547,8 +582,11 @@
             VMEM((8, 128, 128), BF), VMEM((256, 512), F32), VMEM((256, 512), F32),
             VMEM((2, 128, 512), F32), VMEM((4, 512, 512), BF), VMEM((65, 128, 128), F32),
             panel, panel, panel, panel, panel, panel,
-            VMEM((4, 512, 256), BF), VMEM((4, 512, 256), BF), VMEM((3, 256, 128), BF), VMEM((256, 128), BF),
-            VMEM((3, 4, 256, 128), BF), VMEM((4, 256, 128), BF), VMEM((8, 32, 128), BF), VMEM((32, 128), F32),
+            VMEM((4, 512, 256), BF), VMEM((4, 16, 2, 16, 256), BF),
+            VMEM((3, 2, 8, 2, 16, 128), BF), VMEM((3, 16, 16, 256), BF),
+            VMEM((2, 8, 2, 16, 128), BF), VMEM((16, 16, 256), BF),
+            VMEM((3, 8, 16, 128), BF), VMEM((3, 8, 16, 128), BF),
+            VMEM((8, 2, 16, 128), BF), VMEM((8, 2, 16, 128), BF), VMEM((2, 16, 128), F32),
             VMEM((2, 128, 256), BF),
             DMA((12,)), DMA, DMA,
             DMA((2, 8)), DMA((2, 8)),
@@ -559,6 +597,8 @@
             DMA((4,)), DMA((4,)),
             DMA((2, 16)), DMA((2, 16)),
             DMA((16,)), DMA((16,)),
+            DMA((4,)), DMA((4,)),
+            DMA((4,)), DMA((4,)),
             DMA((4,)), DMA((4,)),
             DMA((4,)), DMA((4,)),
             DMA((4,)), DMA((4,)),
@@ -578,7 +618,7 @@
             )
         )
     )
-    return upd, gf.reshape(256, 512), gout[0], gout[1], gout[2], gout[3]
+    return upd, gf.reshape(256, 512), gout[0, 0], gout[0, 1], gout[1, 0], gout[1, 1]
 
 
 def solution(mesh):

time: 111 us -> 105 us (0.946); the launches traced: 110 us -> 105 us
  Pallas kernels: 107 us -> 102 us
    pallas_call x1, Pallas kernels: 107 us -> 102 us  [local(): pl.pallas_call(lambda *refs: layer_kernel(scale, *refs), out_shape=(shape...]
where the time goes in v5:
time: 105 us
  Pallas kernels  102 us (97%)
  local copies, waits for them, and re-layouts  2.11 us (2%)
    pallas_call x1, Pallas kernels, local(): pl.pallas_call(lambda *refs: layer_kernel(scale, *refs), out_shape=(shape...  102 us

profile of v5, /device:TPU:1, one launch (start us, length us, event | category | flops | bytes accessed | tf_op | source)
XLA Modules:
  0.0 105.0 jit_solution(15109040555219808179)
XLA Ops:
  0.6 102.2 %message_passing_layer.1 = (bf16[256,512]{1,0:T(8,128)(2,1)S(1)}, bf16[2,128,512]{2,1,0:T(8,128)(2,1)S(1)}, f32[2,2,32,512]{3,2,1,0:T(8,128)S(1)}) custom-call(bf16[2,128,512]{2,1,0:T(8,128)(2,1)} %bitcast.13, bf16[16,128,128]{2,1,0:T(8,128)(2,1)} %bitcast.12, s32[2,8]{1,0:T(2,128)} %refs_2_.1, bf16[512,512]{1,0:T(8,128)(2,1)} %refs_3_.1, ...), custom_call_target="tpu_custom_call" | custom-call | tf_op jit(solution)/shard_map/message_passing_layer/pallas_call | solution.py:571
  102.9 0.7 slice_bitcast_fusion
  103.6 0.7 copy.16
  104.3 0.7 copy.17

commit v6 on v5

--- a/solution.py
+++ b/solution.py
@@ -13,7 +13,7 @@
 VMEM = pltpu.VMEM
 DMA = pltpu.SemaphoreType.DMA
 HANDED_ALONG_Z = 2
-Y_SUM_AT, X_SUM_AT = 8, 12
+Y_SUM_AT, X_SUM_AT = 11, 14
 
 
 def wrap16(value):

time: 105 us -> 103 us (0.981)
  Pallas kernels: 102 us -> 99.9 us
    pallas_call x1, Pallas kernels: 102 us -> 99.9 us  [local(): pl.pallas_call(lambda *refs: layer_kernel(scale, *refs), out_shape=(shape...]
where the time goes in v6:
time: 103 us
  Pallas kernels  99.9 us (97%)
  local copies, waits for them, and re-layouts  2.11 us (2%)
    pallas_call x1, Pallas kernels, local(): pl.pallas_call(lambda *refs: layer_kernel(scale, *refs), out_shape=(shape...  99.9 us

profile of v6, /device:TPU:1, one launch (start us, length us, event | category | flops | bytes accessed | tf_op | source)
XLA Modules:
  0.0 102.6 jit_solution(3995010809729799552)
XLA Ops:
  0.6 99.9 %message_passing_layer.1 = (bf16[256,512]{1,0:T(8,128)(2,1)S(1)}, bf16[2,128,512]{2,1,0:T(8,128)(2,1)S(1)}, f32[2,2,32,512]{3,2,1,0:T(8,128)S(1)}) custom-call(bf16[2,128,512]{2,1,0:T(8,128)(2,1)} %bitcast.13, bf16[16,128,128]{2,1,0:T(8,128)(2,1)} %bitcast.12, s32[2,8]{1,0:T(2,128)} %refs_2_.1, bf16[512,512]{1,0:T(8,128)(2,1)} %refs_3_.1, ...), custom_call_target="tpu_custom_call" | custom-call | tf_op jit(solution)/shard_map/message_passing_layer/pallas_call | solution.py:571
  100.5 0.7 slice_bitcast_fusion
  101.2 0.7 copy.16
  101.9 0.7 copy.17

commit v7 on v6

--- a/solution.py
+++ b/solution.py
@@ -13,7 +13,7 @@
 VMEM = pltpu.VMEM
 DMA = pltpu.SemaphoreType.DMA
 HANDED_ALONG_Z = 2
-Y_SUM_AT, X_SUM_AT = 11, 14
+Y_SUM_AT, X_SUM_AT = 13, 15
 
 
 def wrap16(value):

time: 103 us -> 103 us (level)
  no operation moved by 1% of the time
where the time goes in v7:
time: 103 us
  Pallas kernels  100 us (97%)
  local copies, waits for them, and re-layouts  2.11 us (2%)
    pallas_call x1, Pallas kernels, local(): pl.pallas_call(lambda *refs: layer_kernel(scale, *refs), out_shape=(shape...  100 us

profile of v7, /device:TPU:1, one launch (start us, length us, event | category | flops | bytes accessed | tf_op | source)
XLA Modules:
  0.0 102.8 jit_solution(2095361455606181333)
XLA Ops:
  0.6 100.0 %message_passing_layer.1 = (bf16[256,512]{1,0:T(8,128)(2,1)S(1)}, bf16[2,128,512]{2,1,0:T(8,128)(2,1)S(1)}, f32[2,2,32,512]{3,2,1,0:T(8,128)S(1)}) custom-call(bf16[2,128,512]{2,1,0:T(8,128)(2,1)} %bitcast.13, bf16[16,128,128]{2,1,0:T(8,128)(2,1)} %bitcast.12, s32[2,8]{1,0:T(2,128)} %refs_2_.1, bf16[512,512]{1,0:T(8,128)(2,1)} %refs_3_.1, ...), custom_call_target="tpu_custom_call" | custom-call | tf_op jit(solution)/shard_map/message_passing_layer/pallas_call | solution.py:571
  100.7 0.7 slice_bitcast_fusion
  101.4 0.7 copy.16
  102.1 0.7 copy.17

commit v8 on v6

--- a/solution.py
+++ b/solution.py
@@ -78,7 +78,7 @@
     tiles_t, cols_t, win, cols_s, keys, table, table_s, aggq, aggr, dagg, delt, self_part, cot_part,
     base, grads, csum, to_next, to_prior, from_prior, from_next, sums, parts,
     half_in, half, a_in, b_in, a_sum, b_sum, a2_in, b2_in, last, rep_in, piece,
-    from_mate, loc, s_mate, r_mate, s1, r1, sx, rx, st, rt, sc, rc, sa, ra, sd, rd,
+    from_mate, delt_t, loc, s_mate, r_mate, s1, r1, sx, rx, st, rt, sc, rc, sa, ra, sd, rd,
     sm, rm, sp, rp, s_core, r_core, s_a, r_a, s_b, r_b, s_a2, r_a2, s_b2, r_b2, s_rep, r_rep, s_row, r_row,
 ):
     g = lax.axis_index("row")
@@ -379,12 +379,14 @@
     for j in range(1, 4):
         delta_arrival(j).wait_recv()
 
+    for i in range(8):
+        delt_t[i] = delt[i].T
     csum[0] = jnp.zeros((128, 128), F32)
 
     def add_tiles(i, running):
         for step in range(4):
             e = table_s[0, i * 4 + step]
-            running = running + dot_at(tiles_t[e], delt[lax.div(e, 8)])
+            running = running + dot(delt_t[lax.div(e, 8)], tiles_t[e])
             csum[i * 4 + step + 1] = running
         return running
 
@@ -512,11 +514,12 @@
 
     for q in range(4):
         cut = slice(q * 128, q * 128 + 128)
-        value = base[:, :, cut]
-        for t in range(4):
-            s = (q // 2) * 8 + 2 * t + q % 2
-            value = value + parts[2 * s : 2 * s + 2].astype(F32)
-        gf[:, :, cut] = value.astype(BF)
+        for half_of in range(2):
+            value = jnp.zeros((128, 128), F32)
+            for t in range(4):
+                s = (q // 2) * 8 + 2 * t + q % 2
+                value = value + parts[2 * s + half_of].astype(F32)
+            gf[half_of, :, cut] = (base[half_of, :, cut] + value.T).astype(BF)
 
     @pl.loop(1, 16)
     def _(o):
@@ -587,7 +590,7 @@
             VMEM((2, 8, 2, 16, 128), BF), VMEM((16, 16, 256), BF),
             VMEM((3, 8, 16, 128), BF), VMEM((3, 8, 16, 128), BF),
             VMEM((8, 2, 16, 128), BF), VMEM((8, 2, 16, 128), BF), VMEM((2, 16, 128), F32),
-            VMEM((2, 128, 256), BF),
+            VMEM((2, 128, 256), BF), VMEM((8, 128, 128), BF),
             DMA((12,)), DMA, DMA,
             DMA((2, 8)), DMA((2, 8)),
             DMA((2, 8, 2)), DMA((2, 8, 2)),

time: 103 us -> 103 us (level)
  no operation moved by 1% of the time
where the time goes in v8:
time: 103 us; the launch traced here: 102 us
  Pallas kernels  99.7 us (97%)
  local copies, waits for them, and re-layouts  2.11 us (2%)
    pallas_call x1, Pallas kernels, local(): pl.pallas_call(lambda *refs: layer_kernel(scale, *refs), out_shape=(shape...  99.7 us

profile of v8, /device:TPU:1, one launch (start us, length us, event | category | flops | bytes accessed | tf_op | source)
XLA Modules:
  0.0 102.5 jit_solution(9108456565906850227)
XLA Ops:
  0.6 99.7 %message_passing_layer.1 = (bf16[256,512]{1,0:T(8,128)(2,1)S(1)}, bf16[2,128,512]{2,1,0:T(8,128)(2,1)S(1)}, f32[2,2,32,512]{3,2,1,0:T(8,128)S(1)}) custom-call(bf16[2,128,512]{2,1,0:T(8,128)(2,1)} %bitcast.13, bf16[16,128,128]{2,1,0:T(8,128)(2,1)} %bitcast.12, s32[2,8]{1,0:T(2,128)} %refs_2_.1, bf16[512,512]{1,0:T(8,128)(2,1)} %refs_3_.1, ...), custom_call_target="tpu_custom_call" | custom-call | tf_op jit(solution)/shard_map/message_passing_layer/pallas_call | solution.py:574
  100.4 0.7 slice_bitcast_fusion
  101.1 0.7 copy.16
  101.8 0.7 copy.17
